TPU v7x, 32 devices: a whole 2x2x4 slice. The times are simulated.
32 devices in a mesh: shard: 4 (over y, core), ctx: 4 (over z), tensor: 2 (over x).
Axes of the slice: x: 2, y: 2, z: 4, core: 2. Of those that a mesh axis runs over, the one named last changes fastest.
Arguments:
- tokens: bfloat16 [4, 2048, 960], P('shard', ('ctx', 'tensor')), may hold values from -6 to 6
- cotangent: bfloat16 [4, 2048, 960], P('shard', ('ctx', 'tensor')), may hold values from -6 to 6
- prenorm_scaling: float32 [960], P('shard'), may hold values from 0.25 to 1.75
- hidden_gain: float32 [960], P('shard'), may hold values from 0.25 to 1.75
- query_weight: bfloat16 [960, 960], P('shard'), may hold values from -0.1875 to 0.1875
- key_matrix: bfloat16 [960, 320], P('shard'), may hold values from -0.1875 to 0.1875
- value_matrix: bfloat16 [960, 320], P('shard'), may hold values from -0.1875 to 0.1875
- output_weight: bfloat16 [960, 960], P('shard'), may hold values from -1.5 to 1.5
- gate_weight: bfloat16 [960, 2560], P('shard', 'tensor'), may hold values from -0.1875 to 0.1875
- up_weight: bfloat16 [960, 2560], P('shard', 'tensor'), may hold values from -0.1875 to 0.1875
- down_weight: bfloat16 [2560, 960], P('tensor', 'shard'), may hold values from -0.3125 to 0.3125
Outputs:
- output: bfloat16 [4, 2048, 960], P('shard', ('ctx', 'tensor'))
- input_grad: float32 [4, 2048, 960], P('shard', ('ctx', 'tensor'))
- attention_gain_grad: float32 [960], P('shard')
- hidden_gain_grad: float32 [960], P('shard')
- query_weight_grad: float32 [960, 960], P('shard')
- key_weight_grad: float32 [960, 320], P('shard')
- value_weight_grad: float32 [960, 320], P('shard')
- output_weight_grad: float32 [960, 960], P('shard')
- gate_weight_grad: float32 [960, 2560], P('shard', 'tensor')
- up_weight_grad: float32 [960, 2560], P('shard', 'tensor')
- down_weight_grad: float32 [2560, 960], P('tensor', 'shard')
All inputs are finite; a program needn't handle non-finite values.
Results may differ from a plain program's by a relative error of at most 0.039.
Values may be sent and summed in bfloat16 or wider, within the bound.
No kernel may reach another device: no remote copies, remote signals or barrier semaphores. Data moves between devices by JAX's collectives and lax.ppermute only.
A program may use at most 128 MiB of HBM per device.

v0:
```python
import math

import jax
import jax.numpy as jnp
from jax import lax
from jax.sharding import PartitionSpec as P

QUERY_HEADS = 15
SHARED_KV_UNITS = 5
ATTN_UNIT_DIM = 64


EPS = 1e-05
THETA = 100000.0
BLOCK = 1024


def rotary_tables(positions, model_width):
    half_width = model_width // 2
    freqs = THETA ** (-(jnp.arange(half_width, dtype=jnp.float32) * 2.0 / model_width))
    angles = positions.astype(jnp.float32)[:, None] * freqs[None, :]
    return (jnp.cos(angles), jnp.sin(angles))


def apply_rotation(value_rows, cosine_table, sine_table):
    half_width = value_rows.shape[-1] // 2
    former = value_rows[..., :half_width]
    latter = value_rows[..., half_width:]
    cos_rows = cosine_table[:, None, :]
    sin_rows = sine_table[:, None, :]
    return jnp.concatenate(
        [former * cos_rows - latter * sin_rows, latter * cos_rows + former * sin_rows], -1
    )


def inverse_rotation(grads, cosine_table, sine_table):
    half_width = grads.shape[-1] // 2
    former = grads[..., :half_width]
    latter = grads[..., half_width:]
    cos_rows = cosine_table[:, None, :]
    sin_rows = sine_table[:, None, :]
    return jnp.concatenate(
        [former * cos_rows + latter * sin_rows, latter * cos_rows - former * sin_rows], -1
    )


def fold_keys(carry, pieces, grouped_heads, positions):
    key_slice, value_slice = pieces
    series_extent = key_slice.shape[0]
    rows_per_block = math.gcd(series_extent, BLOCK)
    block_count = series_extent // rows_per_block
    partitioned_lookups = key_slice.reshape(
        block_count, rows_per_block, SHARED_KV_UNITS, ATTN_UNIT_DIM
    )
    blocked_values = value_slice.reshape(
        block_count, rows_per_block, SHARED_KV_UNITS, ATTN_UNIT_DIM
    )
    scale_factor = ATTN_UNIT_DIM ** (-0.5)

    def fold_advance(state, item):
        key_block, value_block, index = item
        peak_score, totals, accum = state
        key_pos = index * rows_per_block + jnp.arange(rows_per_block, dtype=jnp.int32)
        causal = key_pos[None, :] <= positions[:, None]
        scores = (
            jnp.einsum(
                "qhgd,khd->hgqk", grouped_heads, key_block, preferred_element_type=jnp.float32
            )
            * scale_factor
        )
        scores = jnp.where(causal, scores, -1e30)
        new_peak = jnp.maximum(peak_score, jnp.max(scores, -1))
        rescale = jnp.exp(peak_score - new_peak)
        probs = jnp.where(causal, jnp.exp(scores - new_peak[..., None]), 0.0)
        totals = totals * rescale + jnp.sum(probs, -1)
        accum = accum * rescale[..., None] + jnp.einsum(
            "hgqk,khd->hgqd",
            probs.astype(jnp.bfloat16),
            value_block,
            preferred_element_type=jnp.float32,
        )
        return ((new_peak, totals, accum), None)

    state, unused = lax.scan(
        fold_advance,
        carry,
        (partitioned_lookups, blocked_values, jnp.arange(block_count, dtype=jnp.int32)),
    )
    return state


def shards(
    tokens,
    cotangent,
    prenorm_scaling,
    hidden_gain,
    query_weight,
    key_matrix,
    value_matrix,
    output_weight,
    gate_weight,
    up_weight,
    down_weight,
):
    group_count = QUERY_HEADS // SHARED_KV_UNITS
    token_rows = tokens.shape[1]
    scale_factor = ATTN_UNIT_DIM ** (-0.5)
    place = lax.axis_index(("ctx", "tensor"))
    positions = place * token_rows + jnp.arange(token_rows, dtype=jnp.int32)
    cosine_table, sine_table = rotary_tables(positions, ATTN_UNIT_DIM)
    inputs = tokens[0].astype(jnp.float32)
    full_query, full_key, full_value, full_output, gain_one, gain_two = (
        lax.all_gather(query_weight, "shard", axis=0, tiled=True),
        lax.all_gather(key_matrix, "shard", axis=0, tiled=True),
        lax.all_gather(value_matrix, "shard", axis=0, tiled=True),
        lax.all_gather(output_weight, "shard", axis=0, tiled=True),
        lax.all_gather(prenorm_scaling.astype(jnp.bfloat16), "shard", axis=0, tiled=True).astype(
            prenorm_scaling.dtype
        ),
        lax.all_gather(hidden_gain.astype(jnp.bfloat16), "shard", axis=0, tiled=True).astype(
            hidden_gain.dtype
        ),
    )
    inv_one = lax.rsqrt(jnp.mean(inputs * inputs, -1, keepdims=True) + EPS)
    normed_one = (inputs * inv_one * gain_one).astype(jnp.bfloat16)
    query_projected = jnp.dot(normed_one, full_query, preferred_element_type=jnp.float32)
    key_projected = jnp.dot(normed_one, full_key, preferred_element_type=jnp.float32)
    value_projected = jnp.dot(normed_one, full_value, preferred_element_type=jnp.float32)
    query_rows = apply_rotation(
        query_projected.reshape(token_rows, QUERY_HEADS, ATTN_UNIT_DIM), cosine_table, sine_table
    ).astype(jnp.bfloat16)
    grouped_heads = query_rows.reshape(token_rows, SHARED_KV_UNITS, group_count, ATTN_UNIT_DIM)
    key_rows = (
        apply_rotation(
            key_projected.reshape(token_rows, SHARED_KV_UNITS, ATTN_UNIT_DIM),
            cosine_table,
            sine_table,
        )
        .astype(jnp.bfloat16)
        .reshape(token_rows, SHARED_KV_UNITS * ATTN_UNIT_DIM)
    )
    value_rows = value_projected.astype(jnp.bfloat16)
    initial = (
        jnp.full((SHARED_KV_UNITS, group_count, token_rows), -1e30, jnp.float32),
        jnp.zeros((SHARED_KV_UNITS, group_count, token_rows), jnp.float32),
        jnp.zeros((SHARED_KV_UNITS, group_count, token_rows, ATTN_UNIT_DIM), jnp.float32),
    )
    state = fold_keys(
        initial,
        (
            lax.all_gather(key_rows, ("ctx", "tensor"), axis=0, tiled=True),
            lax.all_gather(value_rows, ("ctx", "tensor"), axis=0, tiled=True),
        ),
        grouped_heads,
        positions,
    )
    peak_score, totals, accum = state
    attended = accum / totals[..., None]
    log_total = peak_score + jnp.log(totals)
    attended_low = (
        attended.transpose(2, 0, 1, 3)
        .reshape(token_rows, QUERY_HEADS * ATTN_UNIT_DIM)
        .astype(jnp.bfloat16)
    )
    branch = jnp.dot(attended_low, full_output, preferred_element_type=jnp.float32)
    hidden_in = inputs + branch
    inv_two = lax.rsqrt(jnp.mean(hidden_in * hidden_in, -1, keepdims=True) + EPS)
    normed_two = (hidden_in * inv_two * gain_two).astype(jnp.bfloat16)
    gate_full, up_full, down_full = (
        lax.all_gather(gate_weight, "shard", axis=0, tiled=True),
        lax.all_gather(up_weight, "shard", axis=0, tiled=True),
        lax.all_gather(down_weight, "shard", axis=1, tiled=True),
    )
    normed_all = lax.all_gather(normed_two, "tensor", axis=0, tiled=True)
    gate_val = jnp.dot(normed_all, gate_full, preferred_element_type=jnp.float32)
    up_val = jnp.dot(normed_all, up_full, preferred_element_type=jnp.float32)
    sigmoid_gate = jax.nn.sigmoid(gate_val)
    product_low = (gate_val * sigmoid_gate * up_val).astype(jnp.bfloat16)
    feed = lax.psum_scatter(
        jnp.dot(product_low, down_full, preferred_element_type=jnp.float32).astype(jnp.bfloat16),
        "tensor",
        scatter_dimension=0,
        tiled=True,
    ).astype(jnp.float32)
    result = (hidden_in + feed).astype(jnp.bfloat16)[None]
    upstream = cotangent[0].astype(jnp.float32)
    upstream_all = lax.all_gather(cotangent[0], "tensor", axis=0, tiled=True)
    d_product = jnp.einsum("td,fd->tf", upstream_all, down_full, preferred_element_type=jnp.float32)
    grad_down = jnp.einsum(
        "tf,td->fd", product_low, upstream_all, preferred_element_type=jnp.float32
    )
    d_up = (d_product * gate_val * sigmoid_gate).astype(jnp.bfloat16)
    d_gate = (d_product * up_val * sigmoid_gate * (1.0 + gate_val * (1.0 - sigmoid_gate))).astype(
        jnp.bfloat16
    )
    grad_gate = jnp.einsum("td,tf->df", normed_all, d_gate, preferred_element_type=jnp.float32)
    grad_up = jnp.einsum("td,tf->df", normed_all, d_up, preferred_element_type=jnp.float32)
    d_normed_two = lax.psum_scatter(
        (
            jnp.einsum("tf,df->td", d_gate, gate_full, preferred_element_type=jnp.float32)
            + jnp.einsum("tf,df->td", d_up, up_full, preferred_element_type=jnp.float32)
        ).astype(jnp.bfloat16),
        "tensor",
        scatter_dimension=0,
        tiled=True,
    ).astype(jnp.float32)
    grad_gain_two = jnp.sum(d_normed_two * hidden_in * inv_two, 0)
    scaled_two = d_normed_two * gain_two
    d_hidden = (
        upstream
        + inv_two * scaled_two
        - hidden_in * inv_two**3 * jnp.mean(scaled_two * hidden_in, -1, keepdims=True)
    )
    d_branch = d_hidden.astype(jnp.bfloat16)
    grad_output = jnp.einsum(
        "te,td->ed", attended_low, d_branch, preferred_element_type=jnp.float32
    )
    attended_grad = jnp.einsum(
        "td,ed->te", d_branch, full_output, preferred_element_type=jnp.float32
    )
    attended_low_grad = attended_grad.astype(jnp.bfloat16).reshape(
        token_rows, SHARED_KV_UNITS, group_count, ATTN_UNIT_DIM
    )
    delta = jnp.einsum(
        "qhgd,hgqd->hgq",
        attended_low_grad.astype(jnp.float32),
        attended,
        preferred_element_type=jnp.float32,
    )
    every_key, every_value = (
        lax.all_gather(key_rows, ("ctx", "tensor"), axis=0, tiled=True),
        lax.all_gather(value_rows, ("ctx", "tensor"), axis=0, tiled=True),
    )
    series_extent = every_key.shape[0]

    def score_grads(key_block, value_block, key_pos):
        causal = key_pos[None, :] <= positions[:, None]
        scores = (
            jnp.einsum(
                "qhgd,khd->hgqk", grouped_heads, key_block, preferred_element_type=jnp.float32
            )
            * scale_factor
        )
        probs = jnp.where(causal, jnp.exp(scores - log_total[..., None]), 0.0)
        d_probs = jnp.einsum(
            "qhgd,khd->hgqk", attended_low_grad, value_block, preferred_element_type=jnp.float32
        )
        d_scores = (scale_factor * probs * (d_probs - delta[..., None])).astype(jnp.bfloat16)
        return (probs, d_scores)

    def key_value_terms(key_block, value_block, key_pos):
        probs, d_scores = score_grads(key_block, value_block, key_pos)
        model_width = key_block.shape[0]
        value_gradient = jnp.einsum(
            "hgqk,qhgd->khd",
            probs.astype(jnp.bfloat16),
            attended_low_grad,
            preferred_element_type=jnp.float32,
        )
        key_gradient = jnp.einsum(
            "hgqk,qhgd->khd", d_scores, grouped_heads, preferred_element_type=jnp.float32
        )
        joined = jnp.concatenate(
            [
                key_gradient.reshape(model_width, SHARED_KV_UNITS * ATTN_UNIT_DIM),
                value_gradient.reshape(model_width, SHARED_KV_UNITS * ATTN_UNIT_DIM),
            ],
            1,
        )
        return (joined, d_scores)

    rows_per_block = math.gcd(series_extent, BLOCK)
    block_count = series_extent // rows_per_block
    partitioned_lookups = every_key.reshape(
        block_count, rows_per_block, SHARED_KV_UNITS, ATTN_UNIT_DIM
    )
    blocked_values = every_value.reshape(
        block_count, rows_per_block, SHARED_KV_UNITS, ATTN_UNIT_DIM
    )
    block_ids = jnp.arange(block_count, dtype=jnp.int32)
    empty_query = jnp.zeros((token_rows, SHARED_KV_UNITS, group_count, ATTN_UNIT_DIM), jnp.float32)

    def body_advance(asker_cotangent, item):
        key_block, value_block, index = item
        key_pos = index * rows_per_block + jnp.arange(rows_per_block, dtype=jnp.int32)
        joined, d_scores = key_value_terms(key_block, value_block, key_pos)
        asker_cotangent = asker_cotangent + jnp.einsum(
            "hgqk,khd->qhgd", d_scores, key_block, preferred_element_type=jnp.float32
        )
        return (asker_cotangent, joined)

    asker_cotangent, lookup_summands = lax.scan(
        body_advance, empty_query, (partitioned_lookups, blocked_values, block_ids)
    )
    key_gradients = lax.psum_scatter(
        lookup_summands.reshape(series_extent, 2 * SHARED_KV_UNITS * ATTN_UNIT_DIM).astype(
            jnp.bfloat16
        ),
        ("ctx", "tensor"),
        scatter_dimension=0,
        tiled=True,
    ).astype(jnp.float32)
    d_key_low = (
        inverse_rotation(
            key_gradients[:, : SHARED_KV_UNITS * ATTN_UNIT_DIM].reshape(
                token_rows, SHARED_KV_UNITS, ATTN_UNIT_DIM
            ),
            cosine_table,
            sine_table,
        )
        .reshape(token_rows, SHARED_KV_UNITS * ATTN_UNIT_DIM)
        .astype(jnp.bfloat16)
    )
    value_low_grad = key_gradients[:, SHARED_KV_UNITS * ATTN_UNIT_DIM :].astype(jnp.bfloat16)
    d_query_low = (
        inverse_rotation(
            asker_cotangent.reshape(token_rows, QUERY_HEADS, ATTN_UNIT_DIM),
            cosine_table,
            sine_table,
        )
        .reshape(token_rows, QUERY_HEADS * ATTN_UNIT_DIM)
        .astype(jnp.bfloat16)
    )
    grad_query = jnp.einsum(
        "td,te->de", normed_one, d_query_low, preferred_element_type=jnp.float32
    )
    grad_key = jnp.einsum("td,te->de", normed_one, d_key_low, preferred_element_type=jnp.float32)
    grad_value = jnp.einsum(
        "td,te->de", normed_one, value_low_grad, preferred_element_type=jnp.float32
    )
    d_normed_one = (
        jnp.einsum("te,de->td", d_query_low, full_query, preferred_element_type=jnp.float32)
        + jnp.einsum("te,de->td", d_key_low, full_key, preferred_element_type=jnp.float32)
        + jnp.einsum("te,de->td", value_low_grad, full_value, preferred_element_type=jnp.float32)
    )
    grad_gain_one = jnp.sum(d_normed_one * inputs * inv_one, 0)
    scaled_one = d_normed_one * gain_one
    d_inputs = (
        d_hidden
        + inv_one * scaled_one
        - inputs * inv_one**3 * jnp.mean(scaled_one * inputs, -1, keepdims=True)
    )
    owned = (
        lax.psum_scatter(
            grad_query.astype(jnp.bfloat16), "shard", scatter_dimension=0, tiled=True
        ).astype(jnp.float32),
        lax.psum_scatter(
            grad_key.astype(jnp.bfloat16), "shard", scatter_dimension=0, tiled=True
        ).astype(jnp.float32),
        lax.psum_scatter(
            grad_value.astype(jnp.bfloat16), "shard", scatter_dimension=0, tiled=True
        ).astype(jnp.float32),
        lax.psum_scatter(
            grad_output.astype(jnp.bfloat16), "shard", scatter_dimension=0, tiled=True
        ).astype(jnp.float32),
        lax.psum_scatter(
            grad_gain_one.astype(jnp.bfloat16), "shard", scatter_dimension=0, tiled=True
        ).astype(jnp.float32),
        lax.psum_scatter(
            grad_gain_two.astype(jnp.bfloat16), "shard", scatter_dimension=0, tiled=True
        ).astype(jnp.float32),
    )
    owned = (
        lax.psum(owned[0].astype(jnp.bfloat16), ("ctx", "tensor")).astype(jnp.float32),
        lax.psum(owned[1].astype(jnp.bfloat16), ("ctx", "tensor")).astype(jnp.float32),
        lax.psum(owned[2].astype(jnp.bfloat16), ("ctx", "tensor")).astype(jnp.float32),
        lax.psum(owned[3].astype(jnp.bfloat16), ("ctx", "tensor")).astype(jnp.float32),
        lax.psum(owned[4].astype(jnp.bfloat16), ("ctx", "tensor")).astype(jnp.float32),
        lax.psum(owned[5].astype(jnp.bfloat16), ("ctx", "tensor")).astype(jnp.float32),
    )
    ffn_owned = (
        lax.psum_scatter(
            grad_gate.astype(jnp.bfloat16), "shard", scatter_dimension=0, tiled=True
        ).astype(jnp.float32),
        lax.psum_scatter(
            grad_up.astype(jnp.bfloat16), "shard", scatter_dimension=0, tiled=True
        ).astype(jnp.float32),
        lax.psum_scatter(
            grad_down.astype(jnp.bfloat16), "shard", scatter_dimension=1, tiled=True
        ).astype(jnp.float32),
    )
    ffn_owned = (
        lax.psum(ffn_owned[0].astype(jnp.bfloat16), "ctx").astype(jnp.float32),
        lax.psum(ffn_owned[1].astype(jnp.bfloat16), "ctx").astype(jnp.float32),
        lax.psum(ffn_owned[2].astype(jnp.bfloat16), "ctx").astype(jnp.float32),
    )
    return (
        result,
        d_inputs[None],
        owned[4],
        owned[5],
        owned[0],
        owned[1],
        owned[2],
        owned[3],
        ffn_owned[0],
        ffn_owned[1],
        ffn_owned[2],
    )


def solution(mesh):
    return jax.shard_map(
        shards,
        mesh=mesh,
        in_specs=(
            P("shard", ("ctx", "tensor"), None),
            P("shard", ("ctx", "tensor"), None),
            P("shard"),
            P("shard"),
            P("shard", None),
            P("shard", None),
            P("shard", None),
            P("shard", None),
            P("shard", "tensor"),
            P("shard", "tensor"),
            P("tensor", "shard"),
        ),
        out_specs=(
            P("shard", ("ctx", "tensor"), None),
            P("shard", ("ctx", "tensor"), None),
            P("shard"),
            P("shard"),
            P("shard", None),
            P("shard", None),
            P("shard", None),
            P("shard", None),
            P("shard", "tensor"),
            P("shard", "tensor"),
            P("tensor", "shard"),
        ),
        check_vma=False,
    )
```

profile of v0, /device:TPU:0, one launch (start us, length us, event | category | flops | bytes accessed | tf_op | source)
XLA Modules:
  0.0 857.6 jit_solution(10382211103331162667)
XLA Ops:
  12.9 8.3 all-reduce.8
  21.3 7.1 all-gather.1
  30.9 8.0 all-gather.2
  44.5 14.3 %all-gather = bf16[1,512,960]{1,2,0:T(8,128)(2,1)} all-gather(bf16[1,256,960]{1,2,0:T(8,128)(2,1)S(1)} %copy-done.20), channel_id=2, replica_groups=mesh['shard'=4,'ctx'=4,'tensor'=2] {'tensor'}, dimensions={1}, use_global_device_ids=true | all-gather | bytes 1474560 | tf_op jit(solution)/shard_map/all_gather | solution.py:187
  58.7 15.9 %all-gather.11.cloned.1.call-done = bf16[2048,320]{0,1:T(8,128)(2,1)} async-done(((bf16[256,320]{0,1:T(8,128)(2,1)}), bf16[2048,320]{0,1:T(8,128)(2,1)}) %all-gather.11.cloned.1.call-update) | async-done | bytes 1310736 | tf_op jit(solution)/shard_map/all_gather | solution.py:151
  74.6 4.4 reshape.252
  80.7 37.5 %all-gather.15.cloned.1.call-done = bf16[2048,320]{0,1:T(8,128)(2,1)} async-done(((bf16[256,320]{0,1:T(8,128)(2,1)}), bf16[2048,320]{0,1:T(8,128)(2,1)}) %all-gather.15.cloned.1.call-update) | async-done | bytes 1310736 | tf_op jit(solution)/shard_map/all_gather | solution.py:152
  118.2 4.4 reshape.253
  122.5 2.8 copy.63
  125.4 14.9 %all-gather.13.cloned.1.call-done = bf16[960,960]{1,0:T(8,128)(2,1)} async-done(((bf16[240,960]{1,0:T(8,128)(2,1)}), bf16[960,960]{1,0:T(8,128)(2,1)}) %all-gather.13.cloned.1.call-update) | async-done | bytes 1843216 | tf_op jit(solution)/shard_map/all_gather | solution.py:113
  140.3 3.8 copy.60
  144.1 2.3 fusion.73
  146.7 51.3 %while.28 = (s32[]{:T(128)}, f32[5,3,256]{2,1,0:T(4,128)S(1)}, f32[5,3,256]{2,1,0:T(4,128)S(1)}, f32[5,3,256,64]{2,3,1,0:T(8,128)S(1)}, s32[2]{0:T(128)S(1)}, /*...) while((s32[]{:T(128)}, f32[5,3,256]{2,1,0:T(4,128)S(1)}, ...), condition=%wide.region_4.5_spmd.clone, body=%wide.region_1.4_spmd.clone.sunk | while | flops 1058770944 | bytes 52258988 | solution.py:84
  148.7 6.8 fusion.158
  155.5 9.3 %fusion.159 = f32[5,3,256]{2,1,0:T(4,128)S(1)} fusion(f32[5,1024,256,3]{2,1,3,0:T(8,128)} %get-tuple-element.476, f32[5,3,256]{2,1,0:T(4,128)S(1)} %select_maximum_fusion.2, pred[256,1024]{0,1:T(8,128)(4,1)S(1)} %broadcast_compare_fusion.4), kind=kLoop, calls=%fused_computation.6.clone.1 | loop fusion | flops 19656960 | bytes 16021504 | tf_op jit(solution)/shard_map/while/body/eval_jaxpr/reduce_sum | solution.py:75
  164.8 7.8 fusion.161
  174.1 6.8 fusion.158
  180.9 9.3 %fusion.159 = f32[5,3,256]{2,1,0:T(4,128)S(1)} fusion(f32[5,1024,256,3]{2,1,3,0:T(8,128)} %get-tuple-element.476, f32[5,3,256]{2,1,0:T(4,128)S(1)} %select_maximum_fusion.2, pred[256,1024]{0,1:T(8,128)(4,1)S(1)} %broadcast_compare_fusion.4), kind=kLoop, calls=%fused_computation.6.clone.1 | loop fusion | flops 19656960 | bytes 16021504 | tf_op jit(solution)/shard_map/while/body/eval_jaxpr/reduce_sum | solution.py:75
  190.2 7.8 fusion.161
  199.0 2.7 multiply_reduce_fusion
  202.8 14.3 %all_gather.49 = bf16[512,960]{0,1:T(8,128)(2,1)S(1)} all-gather(bf16[256,960]{0,1:T(8,128)(2,1)S(1)} %multiply_convert_fusion.3), channel_id=1, replica_groups=mesh['shard'=4,'ctx'=4,'tensor'=2] {'tensor'}, dimensions={0}, use_global_device_ids=true | all-gather | bytes 1474560 | tf_op jit(solution)/shard_map/all_gather | solution.py:174
  217.1 5.1 fusion.93
  222.2 4.9 fusion.92
  227.1 14.9 %all-gather.23.cloned.1.call-done = bf16[1280,960]{0,1:T(8,128)(2,1)} async-done(((bf16[1280,240]{0,1:T(8,128)(2,1)}), bf16[1280,960]{0,1:T(8,128)(2,1)}) %all-gather.23.cloned.1.call-update) | async-done | bytes 2457616 | tf_op jit(solution)/shard_map/all_gather | solution.py:172
  242.0 7.3 multiply_convert_fusion
  251.9 2.4 add_convert_fusion
  254.4 4.6 convolution_convert_fusion.5
  259.1 15.0 %reduce-scatter.17.cloned.1.call-done = bf16[256,960]{0,1:T(8,128)(2,1)} async-done(((bf16[512,960]{0,1:T(8,128)(2,1)}), bf16[256,960]{0,1:T(8,128)(2,1)}) %reduce-scatter.17.cloned.1.call-update) | async-done | bytes 491536 | tf_op jit(solution)/shard_map/reduce_scatter | solution.py:198
  274.1 2.1 fusion.56
  276.2 20.5 %reduce-scatter.15.cloned.1.call-done = bf16[256,960]{0,1:T(8,128)(2,1)} async-done(((bf16[512,960]{0,1:T(8,128)(2,1)}), bf16[256,960]{0,1:T(8,128)(2,1)}) %reduce-scatter.15.cloned.1.call-update) | async-done | bytes 491536 | tf_op jit(solution)/shard_map/reduce_scatter | solution.py:179
  296.7 2.5 fusion.53
  302.8 69.2 %while.29 = (s32[]{:T(128)}, f32[256,5,3,64]{0,3,2,1:T(8,128)}, bf16[2,1024,640]{2,1,0:T(8,128)(2,1)}, bf16[2,1024,5,64]{1,3,2,0:T(8,128)(2,1)S(1)}, s32[2]{0:T(...) while((s32[]{:T(128)}, f32[256,5,3,64]{0,3,2,1:T(8,128)}, ...), condition=%wide.region_10.11_spmd.clone, body=%wide.region_9.10_spmd.clone.sunk | while | flops 2563212544 | bytes 97180928 | solution.py:292
  304.6 7.7 fusion.172
  312.2 8.6 %fusion.175 = bf16[5,1024,64,1]{1,2,3,0:T(8,128)(2,1)S(1)} fusion(bf16[256,5,3,64]{0,3,2,1:T(8,128)(2,1)} %get-tuple-element.562, f32[5,1024,256,3]{2,1,3,0:T(8,128)} %fusion.172, f32[5,3,256]{2,1,0:T(4,128)S(1)} %get-tuple-element.560, pred[256,1024]{0,1:T(8,128)(4,1)S(1)} %broadcast_compare_fusion.5), kind=kOutput, calls=%fused_computation.35.clone.1 | convolution fusion | flops 519045120 | bytes 17153024 | tf_op jit(solution)/shard_map/while/body/eval_jaxpr/hgqk,qhgd->khd/dot_general | solution.py:254
  320.8 8.5 fusion.173
  329.4 2.5 fusion.176
  331.8 2.4 fusion.174
  338.4 7.7 fusion.172
  346.1 8.6 %fusion.175 = bf16[5,1024,64,1]{1,2,3,0:T(8,128)(2,1)S(1)} fusion(bf16[256,5,3,64]{0,3,2,1:T(8,128)(2,1)} %get-tuple-element.562, f32[5,1024,256,3]{2,1,3,0:T(8,128)} %fusion.172, f32[5,3,256]{2,1,0:T(4,128)S(1)} %get-tuple-element.560, pred[256,1024]{0,1:T(8,128)(4,1)S(1)} %broadcast_compare_fusion.5), kind=kOutput, calls=%fused_computation.35.clone.1 | convolution fusion | flops 519045120 | bytes 17153024 | tf_op jit(solution)/shard_map/while/body/eval_jaxpr/hgqk,qhgd->khd/dot_general | solution.py:254
  354.7 8.5 fusion.173
  363.2 2.5 fusion.176
  365.7 3.6 fusion.174
  371.9 4.5 copy.67
  378.0 2.9 convolution_convert_fusion.1
  381.3 4.2 convolution_convert_fusion.2
  385.6 4.3 convolution_convert_fusion
  390.0 57.4 %reduce-scatter.19.cloned.1.call-done = bf16[256,640]{0,1:T(8,128)(2,1)} async-done(((bf16[2048,640]{0,1:T(8,128)(2,1)}), bf16[256,640]{0,1:T(8,128)(2,1)}) %reduce-scatter.19.cloned.1.call-update) | async-done | bytes 327696 | tf_op jit(solution)/shard_map/reduce_scatter | solution.py:295
  452.6 2.0 convolution_convert_fusion.3
  456.8 2.0 convolution_convert_fusion.4
  458.9 23.7 %reduce-scatter.27.cloned.1.call-done = bf16[240,1280]{1,0:T(8,128)(2,1)} async-done(((bf16[960,1280]{1,0:T(8,128)(2,1)}), bf16[240,1280]{1,0:T(8,128)(2,1)}) %reduce-scatter.27.cloned.1.call-update) | async-done | bytes 614416 | tf_op jit(solution)/shard_map/reduce_scatter | solution.py:375
  482.6 36.3 %reduce-scatter.25.cloned.1.call-done = bf16[240,1280]{1,0:T(8,128)(2,1)} async-done(((bf16[960,1280]{1,0:T(8,128)(2,1)}), bf16[240,1280]{1,0:T(8,128)(2,1)}) %reduce-scatter.25.cloned.1.call-update) | async-done | bytes 614416 | tf_op jit(solution)/shard_map/reduce_scatter | solution.py:372
  518.8 36.3 %reduce-scatter.29.cloned.1.call-done = bf16[1280,240]{0,1:T(8,128)(2,1)} async-done(((bf16[1280,960]{0,1:T(8,128)(2,1)}), bf16[1280,240]{0,1:T(8,128)(2,1)}) %reduce-scatter.29.cloned.1.call-update) | async-done | bytes 614416 | tf_op jit(solution)/shard_map/reduce_scatter | solution.py:378
  555.9 25.3 %reduce-scatter.33.cloned.1.call-done = bf16[240,320]{1,0:T(8,128)(2,1)} async-done(((bf16[960,320]{1,0:T(8,128)(2,1)}), bf16[240,320]{1,0:T(8,128)(2,1)}) %reduce-scatter.33.cloned.1.call-update) | async-done | bytes 153616
  582.9 24.2 %reduce-scatter.31.cloned.1.call-done = bf16[240,320]{1,0:T(8,128)(2,1)} async-done(((bf16[960,320]{1,0:T(8,128)(2,1)}), bf16[240,320]{1,0:T(8,128)(2,1)}) %reduce-scatter.31.cloned.1.call-update) | async-done | bytes 153616
  608.9 31.6 %reduce-scatter.23.cloned.1.call-done = bf16[240,960]{1,0:T(8,128)(2,1)} async-done(((bf16[960,960]{1,0:T(8,128)(2,1)}), bf16[240,960]{1,0:T(8,128)(2,1)}) %reduce-scatter.23.cloned.1.call-update) | async-done | bytes 460816 | tf_op jit(solution)/shard_map/reduce_scatter | solution.py:353
  640.4 33.1 %reduce-scatter.21.cloned.1.call-done = bf16[240,960]{1,0:T(8,128)(2,1)} async-done(((bf16[960,960]{1,0:T(8,128)(2,1)}), bf16[240,960]{1,0:T(8,128)(2,1)}) %reduce-scatter.21.cloned.1.call-update) | async-done | bytes 460816 | tf_op jit(solution)/shard_map/reduce_scatter | solution.py:344
  673.6 2.7 fusion.95
  676.2 79.1 %all-reduce.14.cloned.1.call-done = (bf16[240,1280]{1,0:T(8,128)(2,1)}, bf16[240,1280]{1,0:T(8,128)(2,1)}, bf16[1280,240]{0,1:T(8,128)(2,1)}) async-done(((bf16[240,1280]{1,0:T(8,128)(2,1)}, bf16[240,1280]{1,0:T(8,128)(2,1)}, bf16[1280,240]{0,1:T(8,128)(2,1)}), (bf16[240,1280]{1,0:T(8,128)(2,1)}, bf16[240,1280]{1,0:T(8,128)(2,1)}, bf16[1280,240]{0,1:T(8,128)(2,1)})) %all-reduce.14.cloned.1.call-update) | async-done | bytes 1843216 | tf_op jit(solution)/shard_map/psum | solution.py:383
  755.3 2.3 convert_element_type.260
  757.7 2.2 convert_element_type.262
  762.3 6.5 all-reduce.7
  768.9 19.9 %all-reduce.4 = (bf16[240]{0:T(256)(128)(2,1)S(1)}, bf16[240]{0:T(256)(128)(2,1)S(1)}) all-reduce(bf16[240]{0:T(256)(128)(2,1)S(1)} %dynamic-slice.3, bf16[240]{0:T(256)(128)(2,1)S(1)} %dynamic-slice.5), channel_id=1, replica_groups=mesh['shard'=4,'ctx'=4,'tensor'=2] {'ctx','tensor'}, use_global_device_ids=true, to_apply=%region_15.16 | all-reduce | flops 480 | bytes 1920 | tf_op jit(solution)/shard_map/psum | solution.py:368
  791.2 52.9 %all-reduce.12.cloned.1.call-done = (bf16[240,960]{1,0:T(8,128)(2,1)}, bf16[240,320]{0,1:T(8,128)(2,1)}, bf16[240,320]{0,1:T(8,128)(2,1)}, bf16[240,960]{1,0:T(8,128)(2,1)}) async-done(((bf16[240,960]{1,0:T(8,128)(2,1)}, bf16[240,320]{0,1:T(8,128)(2,1)}, bf16[240,320]{0,1:T(8,128)(2,1)}, bf16[240,960]{1,0:T(8,128)(2,1)}), (bf16[240,960]{1,0:T(8,128)(2,1)}, bf16[240,320]{0,1:T(8,128)(2,1)}, ...) | async-done | bytes 1228816 | tf_op jit(solution)/shard_map/psum | solution.py:364
  847.5 2.1 convert_element_type.252
  (228 shorter events, 54.1 us)
Async XLA Ops:
  7.2 22.5 %copy-start.8 = (bf16[1,256,960]{1,2,0:T(8,128)(2,1)S(1)}, bf16[1,256,960]{1,2,0:T(8,128)(2,1)}, u32[]{:S(2)}) copy-start(bf16[1,256,960]{1,2,0:T(8,128)(2,1)} %param.15) | copy-start | bytes 1474564
  7.2 67.4 %all-gather.11.cloned.1.call-start = ((), (), s32[]{:S(2)}) async-start(), calls=%async_computation.10 | async-start | bytes 1474560 | tf_op jit(solution)/shard_map/all_gather | solution.py:151
  10.4 133.7 %copy-start.38 = (f32[256]{0:T(256)}, f32[256]{0:T(256)S(1)}, u32[]{:S(2)}) copy-start(f32[256]{0:T(256)S(1)} %get-tuple-element.352) | copy-start | bytes 3076
  21.3 122.9 %copy-start.36 = (f32[960]{0:T(1024)}, f32[960]{0:T(1024)S(1)}, u32[]{:S(2)}) copy-start(f32[960]{0:T(1024)S(1)} %convert_element_type.217) | copy-start | bytes 11524
  28.3 2.6 copy-start.35
  29.4 1.5 copy-start.12
  29.6 116.9 %copy-start.26 = (f32[256,32]{0,1:T(8,128)}, f32[256,32]{0,1:T(8,128)S(1)}, u32[]{:S(2)}) copy-start(f32[256,32]{0,1:T(8,128)S(1)} %get-tuple-element.349) | copy-start | bytes 98308
  29.6 116.9 %copy-start.28 = (f32[256,32]{0,1:T(8,128)}, f32[256,32]{0,1:T(8,128)S(1)}, u32[]{:S(2)}) copy-start(f32[256,32]{0,1:T(8,128)S(1)} %get-tuple-element.350) | copy-start | bytes 98308
  30.8 87.3 %all-gather.15.cloned.1.call-start = ((), (), s32[]{:S(2)}) async-start(), calls=%async_computation.12 | async-start | bytes 1474560 | tf_op jit(solution)/shard_map/all_gather | solution.py:152
  40.0 18.7 %copy-start.14 = (bf16[960,320]{0,1:T(8,128)(2,1)}, bf16[960,320]{0,1:T(8,128)(2,1)S(1)}, u32[]{:S(2)}) copy-start(bf16[960,320]{0,1:T(8,128)(2,1)S(1)} %reshape.272) | copy-start | bytes 1843204
  40.0 4.5 copy-start.20
  41.1 99.2 %all-gather.13.cloned.1.call-start = ((), (), s32[]{:S(2)}) async-start(), calls=%async_computation.11 | async-start | bytes 2457600 | tf_op jit(solution)/shard_map/all_gather | solution.py:113
  41.9 157.1 %all-gather.17.cloned.1.call-start = ((), (), s32[]{:S(2)}) async-start(), calls=%async_computation.13 | async-start | bytes 2457600 | tf_op jit(solution)/shard_map/all_gather | solution.py:116
  42.5 174.7 %all-gather.21.cloned.1.call-start = ((), (), s32[]{:S(2)}) async-start(), calls=%async_computation.15 | async-start | bytes 3072000 | tf_op jit(solution)/shard_map/all_gather | solution.py:171
  43.0 179.2 %all-gather.19.cloned.1.call-start = ((), (), s32[]{:S(2)}) async-start(), calls=%async_computation.14 | async-start | bytes 3072000 | tf_op jit(solution)/shard_map/all_gather | solution.py:170
  43.6 198.4 %all-gather.23.cloned.1.call-start = ((), (), s32[]{:S(2)}) async-start(), calls=%async_computation.16 | async-start | bytes 3072000 | tf_op jit(solution)/shard_map/all_gather | solution.py:172
  44.4 229.7 %reduce-scatter.17.cloned.1.call-start = ((), (), s32[]{:S(2)}) async-start(), calls=%async_computation.18 | async-start | bytes 1474560 | tf_op jit(solution)/shard_map/reduce_scatter | solution.py:198
  198.0 3.7 copy-start.10
  201.7 0.9 copy-start.6
  217.1 5.1 copy-start.4
  242.0 7.3 copy-start.17
  249.3 1.5 copy-start.44
  249.3 1.5 copy-start.42
  249.3 2.6 copy-start.16
  254.3 42.3 %reduce-scatter.15.cloned.1.call-start = ((), (), s32[]{:S(2)}) async-start(), calls=%async_computation.17 | async-start | bytes 1474560 | tf_op jit(solution)/shard_map/reduce_scatter | solution.py:179
  254.4 19.7 %copy-start.7 = (f32[256,960]{0,1:T(8,128)S(1)}, f32[256,960]{0,1:T(8,128)}, u32[]{:S(2)}) copy-start(f32[256,960]{0,1:T(8,128)} %copy-done.6) | copy-start | bytes 2949124
  259.0 37.7 %copy-start.21 = (bf16[1,256,960]{1,2,0:T(8,128)(2,1)S(1)}, bf16[1,256,960]{1,2,0:T(8,128)(2,1)}, u32[]{:S(2)}) copy-start(bf16[1,256,960]{1,2,0:T(8,128)(2,1)} %param.16) | copy-start | bytes 1474564
  259.0 188.4 %reduce-scatter.19.cloned.1.call-start = ((), (), s32[]{:S(2)}) async-start(), calls=%async_computation.19 | async-start | bytes 2949120 | tf_op jit(solution)/shard_map/reduce_scatter | solution.py:295
  296.7 3.4 copy-start.19
  299.1 2.4 copy-start.11
  303.0 28.8 %copy-start = (bf16[2,1024,5,64]{1,3,2,0:T(8,128)(2,1)}, bf16[2,1024,5,64]{1,3,2,0:T(8,128)(2,1)S(1)}, u32[]{:S(2)}) copy-start(bf16[2,1024,5,64]{1,3,2,0:T(8,128)(2,1)S(1)} %get-tuple-element.557) | copy-start | bytes 3932164 | tf_op jit(solution)/shard_map/while
  335.1 1.8 copy-start.1
  336.9 28.8 %copy-start = (bf16[2,1024,5,64]{1,3,2,0:T(8,128)(2,1)}, bf16[2,1024,5,64]{1,3,2,0:T(8,128)(2,1)S(1)}, u32[]{:S(2)}) copy-start(bf16[2,1024,5,64]{1,3,2,0:T(8,128)(2,1)S(1)} %get-tuple-element.557) | copy-start | bytes 3932164 | tf_op jit(solution)/shard_map/while
  370.1 1.8 copy-start.1
  376.4 1.2 copy-start.5
  376.4 1.6 copy-start.43
  376.5 106.1 %reduce-scatter.27.cloned.1.call-start = ((), (), s32[]{:S(2)}) async-start(), calls=%async_computation.23 | async-start | bytes 3072000 | tf_op jit(solution)/shard_map/reduce_scatter | solution.py:375
  381.0 4.6 copy-start.24
  381.0 137.9 %reduce-scatter.25.cloned.1.call-start = ((), (), s32[]{:S(2)}) async-start(), calls=%async_computation.22 | async-start | bytes 3072000 | tf_op jit(solution)/shard_map/reduce_scatter | solution.py:372
  385.5 61.9 %copy-start.9 = (bf16[1,256,960]{1,2,0:T(8,128)(2,1)S(1)}, bf16[1,256,960]{1,2,0:T(8,128)(2,1)}, u32[]{:S(2)}) copy-start(bf16[1,256,960]{1,2,0:T(8,128)(2,1)} %param.15) | copy-start | bytes 1474564
  385.5 61.9 %copy-start.37 = (f32[960]{0:T(1024)S(1)}, f32[960]{0:T(1024)}, u32[]{:S(2)}) copy-start(f32[960]{0:T(1024)} %copy-done.36) | copy-start | bytes 11524
  385.5 61.9 %copy-start.39 = (f32[256]{0:T(256)S(1)}, f32[256]{0:T(256)}, u32[]{:S(2)}) copy-start(f32[256]{0:T(256)} %copy-done.38) | copy-start | bytes 3076
  385.5 169.6 %reduce-scatter.29.cloned.1.call-start = ((), (), s32[]{:S(2)}) async-start(), calls=%async_computation.24 | async-start | bytes 3072000 | tf_op jit(solution)/shard_map/reduce_scatter | solution.py:378
  389.9 60.2 %copy-start.27 = (f32[256,32]{0,1:T(8,128)S(1)}, f32[256,32]{0,1:T(8,128)}, u32[]{:S(2)}) copy-start(f32[256,32]{0,1:T(8,128)} %copy-done.26) | copy-start | bytes 98308
  390.0 60.2 %copy-start.29 = (f32[256,32]{0,1:T(8,128)S(1)}, f32[256,32]{0,1:T(8,128)}, u32[]{:S(2)}) copy-start(f32[256,32]{0,1:T(8,128)} %copy-done.28) | copy-start | bytes 98308
  390.0 191.2 %reduce-scatter.33.cloned.1.call-start = ((), (), s32[]{:S(2)}) async-start(), calls=%async_computation.26 | async-start | bytes 921600
  447.4 2.7 slice-start
  450.0 2.6 copy-start.3
  450.0 2.6 copy-start.22
  450.0 157.2 %reduce-scatter.31.cloned.1.call-start = ((), (), s32[]{:S(2)}) async-start(), calls=%async_computation.25 | async-start | bytes 921600
  452.5 187.9 %reduce-scatter.23.cloned.1.call-start = ((), (), s32[]{:S(2)}) async-start(), calls=%async_computation.21 | async-start | bytes 2457600 | tf_op jit(solution)/shard_map/reduce_scatter | solution.py:353
  454.6 218.9 %reduce-scatter.21.cloned.1.call-start = ((), (), s32[]{:S(2)}) async-start(), calls=%async_computation.20 | async-start | bytes 2457600 | tf_op jit(solution)/shard_map/reduce_scatter | solution.py:344
  458.8 214.7 %copy-start.18 = (bf16[960,960]{1,0:T(8,128)(2,1)S(1)}, bf16[960,960]{1,0:T(8,128)(2,1)}, u32[]{:S(2)}) copy-start(bf16[960,960]{1,0:T(8,128)(2,1)} %all-gather.13.cloned.1.call-done) | copy-start | bytes 5529604
  458.8 296.5 %all-reduce.14.cloned.1.call-start = ((), (), s32[]{:S(2)}) async-start(), calls=%async_computation.28 | async-start | bytes 3686400 | tf_op jit(solution)/shard_map/psum | solution.py:383
  555.1 288.9 %all-reduce.12.cloned.1.call-start = ((), (), s32[]{:S(2)}) async-start(), calls=%async_computation.27 | async-start | bytes 2621440 | tf_op jit(solution)/shard_map/psum | solution.py:364
  755.3 4.5 copy-start.33
  755.3 5.6 copy-start.13
  755.3 5.6 copy-start.25
  755.3 5.6 copy-start.32
  759.9 1.6 copy-start.15
  759.9 1.6 copy-start.30
  761.0 1.3 copy-start.40
  761.0 29.0 %copy-start.41 = (f32[256]{0:T(256)S(1)}, f32[256]{0:T(256)}, u32[]{:S(2)}) copy-start(f32[256]{0:T(256)} %get-tuple-element.351) | copy-start | bytes 3076
  844.1 5.5 copy-start.34
  (3 other events, 2.4 us)
Sparse Core Ops, SparseCore 0:
  31.0 43.5 all-gather.10
  77.2 40.9 all-gather.14
  119.7 20.5 all-gather.12
  141.7 21.8 all-gather.16
  165.0 24.6 all-gather.20
  191.1 24.6 all-gather.18
  217.3 24.6 all-gather.22
  254.5 19.5 reduce-scatter.16
  277.0 19.5 reduce-scatter.14
  376.6 70.7 reduce-scatter.18
  449.9 32.5 reduce-scatter.26
  485.1 33.6 reduce-scatter.24
  521.4 33.6 reduce-scatter.28
  558.2 22.9 reduce-scatter.32
  584.2 22.9 reduce-scatter.30
  609.8 30.6 reduce-scatter.22
  642.8 30.6 reduce-scatter.20
  676.1 79.1 all-reduce.13
  760.3 83.7 all-reduce.11
where the time goes:
time: 866 us; the launch traced here: 858 us
  waiting for transfers between devices  522 us (60%)
  matrix products  145 us (17%)
  blocking collectives  78.4 us (9%)
  other arithmetic  46.8 us (5%)
  local copies, waits for them, and re-layouts  45.1 us (5%)
  between operations  16.4 us (2%)
    psum x1, waiting for transfers between devices, shards(): lax.psum(ffn_owned[0].astype(jnp.bfloat16), 'ctx').astype(jnp.float32)  79.1 us
    reduce_scatter x1, waiting for transfers between devices, shards(): lax.psum_scatter(lookup_summands.reshape(series_extent, 2 * SHARED_KV_UNI...  57.4 us
    psum x1, waiting for transfers between devices, shards(): lax.psum(owned[0].astype(jnp.bfloat16), ('ctx', 'tensor'))  52.9 us
    unnamed x21, waiting for transfers between devices  52.8 us
    all_gather x1, waiting for transfers between devices, shards(): lax.all_gather(value_rows, ('ctx', 'tensor'), axis=0, tiled=True)  37.5 us
    reduce_scatter x1, waiting for transfers between devices, shards(): lax.psum_scatter(grad_gate.astype(jnp.bfloat16), 'shard', scatter_dimensi...  36.3 us
    reduce_scatter x1, waiting for transfers between devices, shards(): lax.psum_scatter(grad_down.astype(jnp.bfloat16), 'shard', scatter_dimensi...  36.3 us
    reduce_scatter x1, waiting for transfers between devices, shards(): lax.psum_scatter(grad_query.astype(jnp.bfloat16), 'shard', scatter_dimens...  33.1 us
  transfers between devices with their start and end apart: 19, of which 16 were waited for; matrix products, arithmetic and copies ran while one was open for 15% of the time, Pallas kernels for 0%

commit v1 on v0

v1 whole, which is shorter than its diff:
```python
import jax
import jax.numpy as jnp
from jax import lax
from jax.sharding import PartitionSpec as P

QUERY_HEADS = 15
SHARED_KV_UNITS = 5
ATTN_UNIT_DIM = 64
KV_WIDTH = SHARED_KV_UNITS * ATTN_UNIT_DIM
Q_WIDTH = QUERY_HEADS * ATTN_UNIT_DIM

EPS = 1e-05
THETA = 100000.0
F32 = jnp.float32
BF16 = jnp.bfloat16
barrier = lax.optimization_barrier


def rotary_tables(positions, model_width):
    half_width = model_width // 2
    freqs = THETA ** (-(jnp.arange(half_width, dtype=F32) * 2.0 / model_width))
    angles = positions.astype(F32)[:, None] * freqs[None, :]
    return (jnp.cos(angles), jnp.sin(angles))


def apply_rotation(value_rows, cosine_table, sine_table):
    half_width = value_rows.shape[-1] // 2
    former = value_rows[..., :half_width]
    latter = value_rows[..., half_width:]
    cos_rows = cosine_table[:, None, :]
    sin_rows = sine_table[:, None, :]
    return jnp.concatenate(
        [former * cos_rows - latter * sin_rows, latter * cos_rows + former * sin_rows], -1
    )


def inverse_rotation(grads, cosine_table, sine_table):
    return apply_rotation(grads, cosine_table, -sine_table)


def swap_core(block):
    size = lax.axis_size("shard")
    return lax.ppermute(block, "shard", [(i, i ^ 1) for i in range(size)])


def shift_y(block, step):
    size = lax.axis_size("shard")
    return lax.ppermute(block, "shard", [(i, (i + 2 * step) % size) for i in range(size)])


def swap_x(block):
    return lax.ppermute(block, "tensor", [(0, 1), (1, 0)])


def shift_z(block, step):
    size = lax.axis_size("ctx")
    pairs = [(i, i + step) for i in range(size) if 0 <= i + step < size]
    return lax.ppermute(block, "ctx", pairs)


def gather_rows(own, received):
    size = lax.axis_size("shard")
    me = lax.axis_index("shard")
    rows, width = own.shape
    whole = jnp.zeros((size, rows, width), own.dtype)
    for step, block in enumerate([own] + received):
        source = lax.rem(me - 2 * step + size, size)
        other = swap_core(block)
        whole = lax.dynamic_update_slice(whole, block[None], (source, 0, 0))
        whole = lax.dynamic_update_slice(whole, other[None], (jnp.bitwise_xor(source, 1), 0, 0))
    return whole.reshape(size * rows, width)


def from_other_chips(own):
    return [shift_y(own, step) for step in range(1, lax.axis_size("shard") // 2)]


def near_first(columns):
    size = lax.axis_size("shard")
    me = lax.axis_index("shard")
    width = columns.shape[1] // size
    parts = []
    for step in range(size // 2):
        owner = lax.rem(me + 2 * step, size)
        for index in (owner, jnp.bitwise_xor(owner, 1)):
            parts.append(lax.dynamic_slice_in_dim(columns, index * width, width, 1))
    return jnp.concatenate(parts, 1)


def sum_cores(terms):
    size = lax.axis_size("shard")
    split = terms.reshape(size // 2, 2, terms.shape[0] // size, terms.shape[1])
    return split[:, 0].astype(F32) + swap_core(split[:, 1]).astype(F32)


def sum_chips(kept):
    total = kept[0]
    for step in range(1, kept.shape[0]):
        total = total + shift_y(kept[step].astype(BF16), step).astype(F32)
    return total


def sum_ctx(block):
    if lax.axis_size("ctx") != 4:
        return lax.psum(block.astype(BF16), "ctx")
    me = lax.axis_index("ctx")
    inner = jnp.logical_or(me == 1, me == 2)
    edge = lax.ppermute(block.astype(BF16), "ctx", [(0, 1), (3, 2)])
    half = (block.astype(F32) + edge.astype(F32)).astype(BF16)
    swapped = lax.ppermute(half, "ctx", [(1, 2), (2, 1)])
    total = (half.astype(F32) + swapped.astype(F32)).astype(BF16)
    return jnp.where(inner, total, lax.ppermute(total, "ctx", [(1, 0), (2, 3)]))


def halve_x(block):
    half = block.shape[0] // 2
    me = lax.axis_index("tensor")
    kept = lax.dynamic_slice_in_dim(block, me * half, half, 0)
    sent = lax.dynamic_slice_in_dim(block, (1 - me) * half, half, 0)
    return kept + swap_x(sent.astype(BF16)).astype(F32)


def join_x(block):
    other = swap_x(block)
    first = lax.axis_index("tensor") == 0
    return jnp.concatenate(
        [jnp.where(first, block, other), jnp.where(first, other, block)], 0
    ).astype(F32)


def shards(
    tokens,
    cotangent,
    prenorm_scaling,
    hidden_gain,
    query_weight,
    key_matrix,
    value_matrix,
    output_weight,
    gate_weight,
    up_weight,
    down_weight,
):
    group_count = QUERY_HEADS // SHARED_KV_UNITS
    token_rows = tokens.shape[1]
    units = gate_weight.shape[1]
    ctx_size = lax.axis_size("ctx")
    ctx_me = lax.axis_index("ctx")
    tensor_me = lax.axis_index("tensor")
    scale_factor = ATTN_UNIT_DIM ** (-0.5)
    local = jnp.arange(token_rows, dtype=jnp.int32)
    positions = (ctx_me * 2 + tensor_me) * token_rows + local
    cosine_table, sine_table = rotary_tables(positions, ATTN_UNIT_DIM)
    inputs = tokens[0].astype(F32)

    side = jnp.stack([prenorm_scaling, hidden_gain], 1).astype(BF16)
    own_kv = jnp.concatenate([key_matrix, value_matrix, jnp.pad(side, ((0, 0), (0, 62)))], 1)
    own_ffn = jnp.concatenate([gate_weight, up_weight, output_weight], 1)
    own_down = down_weight.T
    far_kv = from_other_chips(own_kv)
    other_cotangent = swap_x(cotangent[0])
    far_kv, query_weight = barrier((far_kv, query_weight))
    far_query = from_other_chips(query_weight)
    first = gather_rows(own_kv, far_kv)
    gains = first[:, 2 * KV_WIDTH :].astype(F32).T
    gain_one, gain_two = gains[0], gains[1]

    inv_one = lax.rsqrt(jnp.mean(inputs * inputs, -1, keepdims=True) + EPS)
    normed_one = (inputs * inv_one * gain_one).astype(BF16)
    projected = jnp.dot(normed_one, first[:, : 2 * KV_WIDTH], preferred_element_type=F32)
    key_rows = (
        apply_rotation(
            projected[:, :KV_WIDTH].reshape(token_rows, SHARED_KV_UNITS, ATTN_UNIT_DIM),
            cosine_table,
            sine_table,
        )
        .astype(BF16)
        .reshape(token_rows, KV_WIDTH)
    )
    value_rows = projected[:, KV_WIDTH:].astype(BF16)
    key_value = jnp.concatenate([key_rows, value_rows], 1)
    far_query, own_ffn, key_value = barrier((far_query, own_ffn, key_value))
    far_ffn = from_other_chips(own_ffn)
    full_query = gather_rows(query_weight, far_query)
    query_projected = jnp.dot(normed_one, full_query, preferred_element_type=F32)
    grouped_heads = (
        apply_rotation(
            query_projected.reshape(token_rows, QUERY_HEADS, ATTN_UNIT_DIM),
            cosine_table,
            sine_table,
        )
        .astype(BF16)
        .reshape(token_rows, SHARED_KV_UNITS, group_count, ATTN_UNIT_DIM)
    )

    def valid_keys(step):
        start = (ctx_me - step) * 2
        key_pos = jnp.concatenate(
            [(start + tensor_me) * token_rows + local, (start + 1 - tensor_me) * token_rows + local]
        )
        return (key_pos[None, :] <= positions[:, None]) & (key_pos[None, :] >= 0)

    def forward_block(state, both, step):
        peak_score, totals, accum = state
        both = both.reshape(2 * token_rows, 2, SHARED_KV_UNITS, ATTN_UNIT_DIM)
        valid = valid_keys(step)
        scores = (
            jnp.einsum("qhgd,khd->hgqk", grouped_heads, both[:, 0], preferred_element_type=F32)
            * scale_factor
        )
        scores = jnp.where(valid, scores, -1e30)
        new_peak = jnp.maximum(peak_score, jnp.max(scores, -1))
        rescale = jnp.exp(peak_score - new_peak)
        probs = jnp.where(valid, jnp.exp(scores - new_peak[..., None]), 0.0)
        totals = totals * rescale + jnp.sum(probs, -1)
        accum = accum * rescale[..., None] + jnp.einsum(
            "hgqk,khd->hgqd", probs.astype(BF16), both[:, 1], preferred_element_type=F32
        )
        return (new_peak, totals, accum)

    state = (
        jnp.full((SHARED_KV_UNITS, group_count, token_rows), -1e30, F32),
        jnp.zeros((SHARED_KV_UNITS, group_count, token_rows), F32),
        jnp.zeros((SHARED_KV_UNITS, group_count, token_rows, ATTN_UNIT_DIM), F32),
    )
    unrolled = ctx_size <= 4
    blocks = []
    passing = key_value
    for step in range(ctx_size):
        if step > 0:
            passing = shift_z(passing, 1)
        both = jnp.concatenate([passing, swap_x(passing)], 0)
        blocks.append(both)
        if unrolled:
            state = forward_block(state, both, step)
    if not unrolled:
        stacked = jnp.stack(blocks)
        steps = jnp.arange(ctx_size, dtype=jnp.int32)
        state, unused = lax.scan(
            lambda held, item: (forward_block(held, item[0], item[1]), None),
            state,
            (stacked, steps),
        )
    peak_score, totals, accum = state
    attended = accum / totals[..., None]
    log_total = peak_score + jnp.log(totals)
    far_ffn, own_down, attended = barrier((far_ffn, own_down, attended))
    far_down = from_other_chips(own_down)
    attended_low = attended.transpose(2, 0, 1, 3).reshape(token_rows, Q_WIDTH).astype(BF16)

    second = gather_rows(own_ffn, far_ffn)
    full_output = second[:, 2 * units :]
    gate_up = second[:, : 2 * units]
    branch = jnp.dot(attended_low, full_output, preferred_element_type=F32)
    hidden_in = inputs + branch
    inv_two = lax.rsqrt(jnp.mean(hidden_in * hidden_in, -1, keepdims=True) + EPS)
    normed_two = (hidden_in * inv_two * gain_two).astype(BF16)
    other_normed = swap_x(normed_two)
    normed_all = jnp.concatenate([normed_two, other_normed], 0)
    upstream_all = jnp.concatenate([cotangent[0], other_cotangent], 0)
    upstream = cotangent[0].astype(F32)
    down_full = gather_rows(own_down, far_down)
    d_product = jnp.dot(upstream_all, down_full, preferred_element_type=F32)
    inner = jnp.dot(normed_all, gate_up, preferred_element_type=F32)
    gate_val = inner[:, :units]
    up_val = inner[:, units:]
    sigmoid_gate = jax.nn.sigmoid(gate_val)
    product_low = (gate_val * sigmoid_gate * up_val).astype(BF16)
    d_up = (d_product * gate_val * sigmoid_gate).astype(BF16)
    d_gate = (d_product * up_val * sigmoid_gate * (1.0 + gate_val * (1.0 - sigmoid_gate))).astype(
        BF16
    )
    d_inner = jnp.concatenate([d_gate, d_up], 1)
    d_normed_sent = jnp.einsum(
        "tf,df->td", d_inner[token_rows:], gate_up, preferred_element_type=F32
    ).astype(BF16)
    d_normed_came = swap_x(d_normed_sent)
    near_normed = near_first(normed_all)
    grad_inner = jnp.einsum(
        "td,tf->df", near_normed, d_inner, preferred_element_type=F32
    ).astype(BF16)
    grad_down = jnp.einsum(
        "td,tf->df", near_first(upstream_all), product_low, preferred_element_type=F32
    ).astype(BF16)
    d_normed_own = jnp.einsum(
        "tf,df->td", d_inner[:token_rows], gate_up, preferred_element_type=F32
    )
    d_normed_came, grad_inner, grad_down, d_normed_own = barrier(
        (d_normed_came, grad_inner, grad_down, d_normed_own)
    )
    d_normed_two = d_normed_own + d_normed_came.astype(F32)
    feed_parts = jnp.einsum("tf,df->td", product_low, down_full, preferred_element_type=F32)
    feed = feed_parts[:token_rows] + swap_x(feed_parts[token_rows:].astype(BF16)).astype(F32)
    result = (hidden_in + feed).astype(BF16)[None]

    grad_gain_two = jnp.sum(d_normed_two * hidden_in * inv_two, 0)
    scaled_two = d_normed_two * gain_two
    d_hidden = (
        upstream
        + inv_two * scaled_two
        - hidden_in * inv_two**3 * jnp.mean(scaled_two * hidden_in, -1, keepdims=True)
    )
    d_branch = d_hidden.astype(BF16)
    attended_grad = jnp.einsum("td,ed->te", d_branch, full_output, preferred_element_type=F32)
    grad_output = jnp.einsum(
        "te,td->ed", near_first(attended_low), d_branch, preferred_element_type=F32
    ).astype(BF16)
    attended_low_grad = attended_grad.astype(BF16)
    attended_low_grad, grad_output, grad_inner, grad_down = barrier(
        (attended_low_grad, grad_output, grad_inner, grad_down)
    )
    attended_low_grad = attended_low_grad.reshape(
        token_rows, SHARED_KV_UNITS, group_count, ATTN_UNIT_DIM
    )

    down_total = sum_chips(sum_cores(grad_down))
    inner_total = sum_chips(sum_cores(grad_inner))
    output_total = sum_chips(sum_cores(grad_output))
    out_down = sum_ctx(down_total).T.astype(F32)
    out_gate = sum_ctx(inner_total[:, :units]).astype(F32)
    out_up = sum_ctx(inner_total[:, units:]).astype(F32)
    out_output = join_x(sum_ctx(halve_x(output_total)))

    delta = jnp.einsum(
        "qhgd,hgqd->hgq", attended_low_grad.astype(F32), attended, preferred_element_type=F32
    )

    def backward_block(asker_cotangent, both, step):
        both = both.reshape(2 * token_rows, 2, SHARED_KV_UNITS, ATTN_UNIT_DIM)
        valid = valid_keys(step)
        scores = (
            jnp.einsum("qhgd,khd->hgqk", grouped_heads, both[:, 0], preferred_element_type=F32)
            * scale_factor
        )
        probs = jnp.where(valid, jnp.exp(scores - log_total[..., None]), 0.0)
        d_probs = jnp.einsum(
            "qhgd,khd->hgqk", attended_low_grad, both[:, 1], preferred_element_type=F32
        )
        d_scores = (scale_factor * probs * (d_probs - delta[..., None])).astype(BF16)
        value_gradient = jnp.einsum(
            "hgqk,qhgd->khd", probs.astype(BF16), attended_low_grad, preferred_element_type=F32
        )
        key_gradient = jnp.einsum(
            "hgqk,qhgd->khd", d_scores, grouped_heads, preferred_element_type=F32
        )
        asker_cotangent = asker_cotangent + jnp.einsum(
            "hgqk,khd->qhgd", d_scores, both[:, 0], preferred_element_type=F32
        )
        joined = jnp.concatenate(
            [
                key_gradient.reshape(2 * token_rows, KV_WIDTH),
                value_gradient.reshape(2 * token_rows, KV_WIDTH),
            ],
            1,
        )
        return asker_cotangent, joined

    asker_cotangent = jnp.zeros((token_rows, SHARED_KV_UNITS, group_count, ATTN_UNIT_DIM), F32)
    if not unrolled:
        asker_cotangent, terms = lax.scan(
            lambda held, item: backward_block(held, item[0], item[1]),
            asker_cotangent,
            (stacked, steps),
        )
    arriving = None
    for step in reversed(range(ctx_size)):
        if unrolled:
            asker_cotangent, joined = backward_block(asker_cotangent, blocks[step], step)
        else:
            joined = terms[step]
        part = joined[:token_rows] + swap_x(joined[token_rows:].astype(BF16)).astype(F32)
        if arriving is not None:
            part = part + arriving.astype(F32)
        if step > 0:
            arriving = shift_z(part.astype(BF16), -1)
    key_value_grad = part
    d_query_low = (
        inverse_rotation(
            asker_cotangent.reshape(token_rows, QUERY_HEADS, ATTN_UNIT_DIM),
            cosine_table,
            sine_table,
        )
        .reshape(token_rows, Q_WIDTH)
        .astype(BF16)
    )
    near_one = near_first(normed_one)
    grad_query = jnp.einsum(
        "td,te->de", near_one, d_query_low, preferred_element_type=F32
    ).astype(BF16)
    query_total = sum_chips(sum_cores(grad_query))
    out_query = join_x(sum_ctx(halve_x(query_total)))
    d_normed_query = jnp.einsum("te,de->td", d_query_low, full_query, preferred_element_type=F32)
    d_key_low = (
        inverse_rotation(
            key_value_grad[:, :KV_WIDTH].reshape(token_rows, SHARED_KV_UNITS, ATTN_UNIT_DIM),
            cosine_table,
            sine_table,
        )
        .reshape(token_rows, KV_WIDTH)
        .astype(BF16)
    )
    value_low_grad = key_value_grad[:, KV_WIDTH:].astype(BF16)
    d_projected = jnp.concatenate([d_key_low, value_low_grad], 1)
    grad_kv = jnp.einsum(
        "td,te->de", near_one, d_projected, preferred_element_type=F32
    ).astype(BF16)
    d_normed_one = d_normed_query + jnp.einsum(
        "te,de->td", d_projected, first[:, : 2 * KV_WIDTH], preferred_element_type=F32
    )
    grad_gain_one = jnp.sum(d_normed_one * inputs * inv_one, 0)
    scaled_one = d_normed_one * gain_one
    d_inputs = (
        d_hidden
        + inv_one * scaled_one
        - inputs * inv_one**3 * jnp.mean(scaled_one * inputs, -1, keepdims=True)
    )
    gain_grads = near_first(jnp.stack([grad_gain_one, grad_gain_two], 0)).T.astype(BF16)
    last = jnp.concatenate([grad_kv, jnp.pad(gain_grads, ((0, 0), (0, 62)))], 1)
    last = join_x(sum_ctx(halve_x(sum_chips(sum_cores(last)))))
    return (
        result,
        d_inputs[None],
        last[:, 2 * KV_WIDTH],
        last[:, 2 * KV_WIDTH + 1],
        out_query,
        last[:, :KV_WIDTH],
        last[:, KV_WIDTH : 2 * KV_WIDTH],
        out_output,
        out_gate,
        out_up,
        out_down,
    )


def solution(mesh):
    return jax.shard_map(
        shards,
        mesh=mesh,
        in_specs=(
            P("shard", ("ctx", "tensor"), None),
            P("shard", ("ctx", "tensor"), None),
            P("shard"),
            P("shard"),
            P("shard", None),
            P("shard", None),
            P("shard", None),
            P("shard", None),
            P("shard", "tensor"),
            P("shard", "tensor"),
            P("tensor", "shard"),
        ),
        out_specs=(
            P("shard", ("ctx", "tensor"), None),
            P("shard", ("ctx", "tensor"), None),
            P("shard"),
            P("shard"),
            P("shard", None),
            P("shard", None),
            P("shard", None),
            P("shard", None),
            P("shard", "tensor"),
            P("shard", "tensor"),
            P("tensor", "shard"),
        ),
        check_vma=False,
    )
```

time: 866 us -> 456 us (0.53)
  waiting for transfers between devices: 522 us -> 155 us
  blocking collectives: 78.4 us -> 0 us
  starting transfers between devices: 1.02 us -> 74 us
  matrix products: 145 us -> 110 us
  between operations: 16.4 us -> 3.08 us
    reduce_scatter x8 -> x0, waiting for transfers between devices: 254 us -> none  [the longest x1 57.4 us: shards(): lax.psum_scatter(lookup_summands.reshape(series_extent, 2 * SHARED_KV_UNI...]
    ppermute x0 -> x64, waiting for transfers between devices: none -> 155 us  [the longest x18 52.4 us: swap_x(): return lax.ppermute(block, 'tensor', [(0, 1), (1, 0)])]
    psum x2 -> x0, waiting for transfers between devices: 132 us -> none  [the longest x1 79.1 us: shards(): lax.psum(ffn_owned[0].astype(jnp.bfloat16), 'ctx').astype(jnp.float32)]
    all_gather x7 -> x0, waiting for transfers between devices: 83.1 us -> none  [the longest x1 37.5 us: shards(): lax.all_gather(value_rows, ('ctx', 'tensor'), axis=0, tiled=True)]
    ppermute x0 -> x64, starting transfers between devices: none -> 74 us  [the longest x18 19.3 us: swap_x(): return lax.ppermute(block, 'tensor', [(0, 1), (1, 0)])]
    unnamed x21 -> x0, waiting for transfers between devices: 52.8 us -> none
    all_gather x4 -> x0, blocking collectives: 43.6 us -> none  [the longest x1 14.3 us: shards(): normed_all = lax.all_gather(normed_two, 'tensor', axis=0, tiled=True)]
    dot_general x35 -> x40, matrix products: 145 us -> 110 us  [the longest x4 17.6 us: forward_block(): jnp.einsum('qhgd,khd->hgqk', grouped_heads, both[:, 0], preferred_element...]
  transfers between devices with their start and end apart: 19 -> 64, of which waited for: 16 -> 23; matrix products, arithmetic and copies ran while one was open for 15% -> 34% of each run, Pallas kernels for 0% -> 0%
where the time goes in v1:
time: 456 us; the launch traced here: 447 us
  waiting for transfers between devices  155 us (34%)
  matrix products  110 us (24%)
  starting transfers between devices  74 us (16%)
  other arithmetic  55.1 us (12%)
  local copies, waits for them, and re-layouts  50 us (11%)
    ppermute x18, waiting for transfers between devices, swap_x(): return lax.ppermute(block, 'tensor', [(0, 1), (1, 0)])  52.4 us
    ppermute x6, waiting for transfers between devices, sum_ctx(): return jnp.where(inner, total, lax.ppermute(total, 'ctx', [(1, 0), (2, 3)]))  49.2 us
    ppermute x9, waiting for transfers between devices, shift_y(): lax.ppermute(block, 'shard', [(i, (i + 2 * step) % size) for i in range(s...  21.8 us
    ppermute x18, starting transfers between devices, swap_x(): return lax.ppermute(block, 'tensor', [(0, 1), (1, 0)])  19.3 us
    ppermute x6, waiting for transfers between devices, sum_ctx(): edge = lax.ppermute(block.astype(BF16), 'ctx', [(0, 1), (3, 2)])  18.5 us
    dot_general x4, matrix products, forward_block(): jnp.einsum('qhgd,khd->hgqk', grouped_heads, both[:, 0], preferred_element...  17.6 us
    dot_general x4, matrix products, backward_block(): jnp.einsum('qhgd,khd->hgqk', attended_low_grad, both[:, 1], preferred_ele...  15.2 us
    ppermute x6, starting transfers between devices, shift_z(): return lax.ppermute(block, 'ctx', pairs)  14.9 us
  transfers between devices with their start and end apart: 64, of which 23 were waited for; matrix products, arithmetic and copies ran while one was open for 34% of the time, Pallas kernels for 0%

profile of v1, /device:TPU:0, one launch (start us, length us, event | category | flops | bytes accessed | tf_op | source)
XLA Modules:
  0.0 447.3 jit_solution(9246965095587070614)
XLA Ops:
  4.4 2.5 collective-permute-start
  28.7 1.9 fusion.114
  39.5 4.2 collective-permute-start.8
  44.2 3.4 broadcast_in_dim.184
  53.3 3.6 collective-permute-start.10
  57.9 2.6 copy.146
  60.5 2.4 fusion.175
  63.1 5.1 %fusion.16 = (f32[5,3,256]{2,1,0:T(4,128)}, f32[5,512,256,3]{2,1,3,0:T(8,128)}) fusion(pred[256,512]{0,1:T(8,128)(4,1)S(1)} %copy-done.42, bf16[256,5,3,32]{0,3,2,1:T(8,128)(2,1)S(1)} %bitcast.471, bf16[256,5,3,32]{0,3,2,1:T(8,128)(2,1)S(1)} %bitcast.463, bf16[512,2,5,64]{0,3,2,1:T(8,128)(2,1)S(1)} %bitcast.503), kind=kOutput, calls=%fused_computation.32 | convolution fusion | flops 258535680 | bytes 8829952 | tf_op jit(solution)/shard_map/qhgd,khd->hgqk/dot_general | solution.py:208
  71.2 2.9 collective-permute-start.12
  74.1 5.1 %fusion.17 = (f32[5,3,256]{2,1,0:T(4,128)}, f32[5,512,256,3]{2,1,3,0:T(8,128)}) fusion(pred[256,512]{0,1:T(8,128)(4,1)S(1)} %copy-done.39, bf16[256,5,3,32]{0,3,2,1:T(8,128)(2,1)S(1)} %bitcast.472, bf16[256,5,3,32]{0,3,2,1:T(8,128)(2,1)S(1)} %bitcast.464, bf16[512,2,5,64]{0,3,2,1:T(8,128)(2,1)S(1)} %bitcast.507), kind=kOutput, calls=%fused_computation.33 | convolution fusion | flops 258535680 | bytes 8829952 | tf_op jit(solution)/shard_map/qhgd,khd->hgqk/dot_general | solution.py:208
  81.8 5.1 %fusion.18 = (f32[5,3,256]{2,1,0:T(4,128)}, f32[5,512,256,3]{2,1,3,0:T(8,128)}) fusion(pred[256,512]{0,1:T(8,128)(4,1)S(1)} %copy-done.36, bf16[256,5,3,32]{0,3,2,1:T(8,128)(2,1)S(1)} %bitcast.473, bf16[256,5,3,32]{0,3,2,1:T(8,128)(2,1)S(1)} %bitcast.465, bf16[512,2,5,64]{0,3,2,1:T(8,128)(2,1)S(1)} %bitcast.511), kind=kOutput, calls=%fused_computation.34 | convolution fusion | flops 258535680 | bytes 8829952 | tf_op jit(solution)/shard_map/qhgd,khd->hgqk/dot_general | solution.py:208
  86.9 2.2 collective-permute-done.13
  90.3 2.3 fusion.19
  92.7 5.3 %fusion.26 = f32[5,3,256]{2,1,0:T(4,128)S(1)} fusion(f32[5,512,256,3]{2,1,3,0:T(8,128)} %get-tuple-element.126, f32[5,3,256]{2,1,0:T(4,128)S(1)} %get-tuple-element.56, pred[256,512]{0,1:T(8,128)(4,1)S(1)} %copy-done.40), kind=kLoop, calls=%fused_computation.42 | loop fusion | flops 9826560 | bytes 8026112 | tf_op jit(solution)/shard_map/reduce_sum | solution.py:215
  98.0 5.3 %fusion.44 = f32[5,3,256,64]{2,3,1,0:T(8,128)S(1)} fusion(f32[5,512,256,3]{2,1,3,0:T(8,128)} %get-tuple-element.126, f32[5,3,256]{2,1,0:T(4,128)S(1)} %get-tuple-element.56, pred[256,512]{0,1:T(8,128)(4,1)S(1)} %copy-done.40, bf16[512,2,5,64]{0,3,2,1:T(8,128)(2,1)S(1)} %bitcast.508), kind=kOutput, calls=%fused_computation.56 | convolution fusion | flops 261488640 | bytes 9326592 | tf_op jit(solution)/shard_map/hgqk,khd->hgqd/dot_general | solution.py:216
  103.4 1.9 fusion.28
  105.3 2.4 fusion.42
  107.8 1.9 fusion.24
  109.7 1.9 fusion.30
  112.2 2.0 fusion.40
  114.3 2.3 fusion.147
  118.4 2.8 bitcast_dynamic-update-slice_fusion.2
  121.2 2.8 bitcast_dynamic-update-slice_fusion.1
  125.1 7.9 %collective-permute-done.18 = bf16[240,1280]{1,0:T(8,128)(2,1)S(1)} collective-permute-done((bf16[240,1280]{1,0:T(8,128)(2,1)S(1)}, bf16[240,1280]{1,0:T(8,128)(2,1)S(1)}, u32[]{:S(2)}, u32[]{:S(2)}) %collective-permute-start.18) | collective-permute-done | bytes 614432 | tf_op jit(solution)/shard_map/ppermute | solution.py:48
  134.4 2.5 multiply_reduce_fusion.2
  138.3 12.6 %collective-permute-done.16 = bf16[256,960]{0,1:T(8,128)(2,1)S(1)} collective-permute-done((bf16[256,960]{0,1:T(8,128)(2,1)S(1)}, bf16[256,960]{0,1:T(8,128)(2,1)S(1)}, u32[]{:S(2)}, u32[]{:S(2)}) %collective-permute-start.16) | collective-permute-done | bytes 491552 | tf_op jit(solution)/shard_map/ppermute | solution.py:52
  150.8 4.9 %fusion.60 = f32[512,2560]{1,0:T(8,128)S(1)} fusion(bf16[960,3520]{1,0:T(8,128)(2,1)} %bitcast.60, bf16[256,960]{0,1:T(8,128)(2,1)S(1)} %collective-permute-done.16, bf16[256,960]{0,1:T(8,128)(2,1)S(1)} %multiply_convert_fusion.3), kind=kOutput, calls=%fused_computation.70 | convolution fusion | flops 2518548480 | bytes 11141120 | tf_op jit(solution)/shard_map/dot_general | solution.py:264
  155.7 4.3 multiply_convert_fusion
  160.0 4.4 fusion.56
  164.5 4.7 %fusion.100 = bf16[256,960]{0,1:T(8,128)(2,1)} fusion(bf16[960,3520]{1,0:T(8,128)(2,1)} %bitcast.60, bf16[512,1280]{1,0:T(8,128)(2,1)S(1)} %copy-done.82, bf16[512,1280]{1,0:T(8,128)(2,1)S(1)} %copy-done.81), kind=kOutput, calls=%fused_computation.147 | convolution fusion | flops 1261158400 | bytes 8028160 | tf_op jit(solution)/shard_map/tf,df->td/dot_general | solution.py:274
  173.0 6.8 %convolution_convert_fusion = bf16[960,2560]{1,0:T(8,128)(2,1)} fusion(bf16[512,1280]{1,0:T(8,128)(2,1)} %get-tuple-element.57, bf16[512,1280]{1,0:T(8,128)(2,1)} %get-tuple-element.58, bf16[512,240]{0,1:T(8,128)(2,1)S(1)} %get-tuple-element.79, bf16[512,240]{0,1:T(8,128)(2,1)S(1)} %get-tuple-element.78, bf16[512,240]{0,1:T(8,128)(2,1)S(1)} %get-tuple-element.77, ...), kind=kOutput, calls=%fused_computation.48 | convolution fusion | flops 2528215040 | bytes 8519680 | tf_op jit(solution)/shard_map/td,tf->df/dot_general | solution.py:279
  179.8 4.2 convolution_convert_fusion.1
  184.0 10.2 %collective-permute-done.22 = bf16[256,960]{0,1:T(8,128)(2,1)S(1)} collective-permute-done((bf16[256,960]{0,1:T(8,128)(2,1)}, bf16[256,960]{0,1:T(8,128)(2,1)S(1)}, u32[]{:S(2)}, u32[]{:S(2)}) %collective-permute-start.22) | collective-permute-done | bytes 491552 | tf_op jit(solution)/shard_map/ppermute | solution.py:52
  196.5 2.6 fusion.97
  199.2 2.0 convolution_convert_fusion.3
  201.2 2.5 fusion.38
  203.7 2.5 fusion.36
  207.1 5.3 %fusion.1 = bf16[5,3,256,512]{2,3,1,0:T(8,128)(2,1)} fusion(f32[5,512,256,3]{2,1,3,0:T(8,128)S(1)} %bitcast.458, f32[5,3,256]{2,1,0:T(4,128)} %fusion.146, f32[5,3,256]{2,1,0:T(4,128)} %get-tuple-element.49, pred[256,512]{0,1:T(8,128)(4,1)S(1)} %copy-done.44, bf16[256,5,3,64]{0,3,2,1:T(8,128)(2,1)} %bitcast.548, bf16[512,2,5,64]{0,3,2,1:T(8,128)(2,1)S(1)} %bitcast.505), kind=kOutput, calls=%fused_computation.2 | convolution fusion | flops 265420800 | bytes 12777472 | tf_op jit(solution)/shard_map/qhgd,khd->hgqk/dot_general | solution.py:336
  212.4 3.9 fusion.3
  216.4 2.5 fusion.34
  218.9 2.8 fusion.5
  223.3 3.2 fusion.7
  242.0 8.4 %collective-permute-done.26 = bf16[256,640]{0,1:T(8,128)(2,1)S(1)} collective-permute-done((bf16[256,640]{0,1:T(8,128)(2,1)S(1)}, bf16[256,640]{0,1:T(8,128)(2,1)S(1)}, u32[]{:S(2)}, u32[]{:S(2)}) %collective-permute-start.26) | collective-permute-done | bytes 327712 | tf_op jit(solution)/shard_map/ppermute | solution.py:52
  253.4 8.1 %collective-permute-done.27 = bf16[256,640]{0,1:T(8,128)(2,1)S(1)} collective-permute-done((bf16[256,640]{0,1:T(8,128)(2,1)S(1)}, bf16[256,640]{0,1:T(8,128)(2,1)S(1)}, u32[]{:S(2)}, u32[]{:S(2)}) %collective-permute-start.27) | collective-permute-done | bytes 327712 | tf_op jit(solution)/shard_map/ppermute | solution.py:58
  267.7 8.9 %collective-permute-done.24 = bf16[256,640]{0,1:T(8,128)(2,1)S(1)} collective-permute-done((bf16[256,640]{0,1:T(8,128)(2,1)S(1)}, bf16[256,640]{0,1:T(8,128)(2,1)S(1)}, u32[]{:S(2)}, u32[]{:S(2)}) %collective-permute-start.24) | collective-permute-done | bytes 327712 | tf_op jit(solution)/shard_map/ppermute | solution.py:52
  282.9 4.9 %collective-permute-done.29 = bf16[256,640]{0,1:T(8,128)(2,1)S(1)} collective-permute-done((bf16[256,640]{0,1:T(8,128)(2,1)S(1)}, bf16[256,640]{0,1:T(8,128)(2,1)S(1)}, u32[]{:S(2)}, u32[]{:S(2)}) %collective-permute-start.29) | collective-permute-done | bytes 327712 | tf_op jit(solution)/shard_map/ppermute | solution.py:58
  297.2 2.2 copy.216
  299.5 2.6 fusion.121
  308.5 5.4 %collective-permute-done.46 = bf16[120,960]{1,0:T(8,128)(2,1)S(1)} collective-permute-done((bf16[120,960]{1,0:T(8,128)(2,1)S(1)}, bf16[120,960]{1,0:T(8,128)(2,1)S(1)}, u32[]{:S(2)}, u32[]{:S(2)}) %collective-permute-start.46) | collective-permute-done | bytes 230432 | tf_op jit(solution)/shard_map/ppermute | solution.py:52
  314.0 3.6 collective-permute-start.47
  318.8 3.6 collective-permute-start.40
  326.1 2.7 collective-permute-done.40
  335.4 9.0 %collective-permute-done.49 = bf16[120,960]{1,0:T(8,128)(2,1)S(1)} collective-permute-done((bf16[120,960]{1,0:T(8,128)(2,1)S(1)}, bf16[120,960]{1,0:T(8,128)(2,1)S(1)}, u32[]{:S(2)}, u32[]{:S(2)}) %collective-permute-start.49) | collective-permute-done | bytes 230432 | tf_op jit(solution)/shard_map/ppermute | solution.py:112
  345.1 2.0 collective-permute-done.42
  349.5 2.4 convert_add_fusion
  355.0 3.4 collective-permute-done.32
  360.1 2.9 collective-permute-done.33
  363.9 13.7 %collective-permute-done.52 = bf16[240,2560]{1,0:T(8,128)(2,1)S(1)} collective-permute-done((bf16[240,2560]{1,0:T(8,128)(2,1)S(1)}, bf16[240,2560]{1,0:T(8,128)(2,1)S(1)}, u32[]{:S(2)}, u32[]{:S(2)}) %collective-permute-start.52) | collective-permute-done | bytes 1228832 | tf_op jit(solution)/shard_map/ppermute | solution.py:48
  384.4 4.0 collective-permute-done.35
  389.0 4.8 %collective-permute-done.53 = bf16[240,1280]{1,0:T(8,128)(2,1)S(1)} collective-permute-done((bf16[240,1280]{1,0:T(8,128)(2,1)S(1)}, bf16[240,1280]{1,0:T(8,128)(2,1)S(1)}, u32[]{:S(2)}, u32[]{:S(2)}) %collective-permute-start.53) | collective-permute-done | bytes 614432 | tf_op jit(solution)/shard_map/ppermute | solution.py:108
  393.8 8.0 %collective-permute-done.56 = bf16[240,1280]{1,0:T(8,128)(2,1)S(1)} collective-permute-done((bf16[240,1280]{1,0:T(8,128)(2,1)S(1)}, bf16[240,1280]{1,0:T(8,128)(2,1)S(1)}, u32[]{:S(2)}, u32[]{:S(2)}) %collective-permute-start.56) | collective-permute-done | bytes 614432 | tf_op jit(solution)/shard_map/ppermute | solution.py:108
  409.6 10.7 %collective-permute-done.63 = bf16[240,1280]{1,0:T(8,128)(2,1)S(1)} collective-permute-done((bf16[240,1280]{1,0:T(8,128)(2,1)S(1)}, bf16[240,1280]{1,0:T(8,128)(2,1)S(1)}, u32[]{:S(2)}, u32[]{:S(2)}) %collective-permute-start.63) | collective-permute-done | bytes 614432 | tf_op jit(solution)/shard_map/ppermute | solution.py:112
  421.5 17.6 %collective-permute-done.58 = bf16[240,1280]{1,0:T(8,128)(2,1)S(1)} collective-permute-done((bf16[240,1280]{1,0:T(8,128)(2,1)S(1)}, bf16[240,1280]{1,0:T(8,128)(2,1)S(1)}, u32[]{:S(2)}, u32[]{:S(2)}) %collective-permute-start.58) | collective-permute-done | bytes 614432 | tf_op jit(solution)/shard_map/ppermute | solution.py:112
  440.2 5.9 %collective-permute-done.55 = bf16[240,1280]{1,0:T(8,128)(2,1)S(1)} collective-permute-done((bf16[240,1280]{1,0:T(8,128)(2,1)S(1)}, bf16[240,1280]{1,0:T(8,128)(2,1)S(1)}, u32[]{:S(2)}, u32[]{:S(2)}) %collective-permute-start.55) | collective-permute-done | bytes 614432 | tf_op jit(solution)/shard_map/ppermute | solution.py:112
  (455 shorter events, 147.7 us)
Async XLA Ops:
  4.0 14.1 %collective-permute-start.2 = (bf16[240,704]{0,1:T(8,128)(2,1)}, bf16[240,704]{0,1:T(8,128)(2,1)}, u32[]{:S(2)}, u32[]{:S(2)}) collective-permute-start(bf16[240,704]{0,1:T(8,128)(2,1)} %get-tuple-element.103), channel_id=1, source_target_pairs={{0,8},{8,0},{16,24},{24,16},{1,9},{9,1},{17,25},{25,17},{2,10},{10... | collective-permute-start | bytes 1013768 | tf_op jit(solution)/shard_map/ppermute | solution.py:43
  4.4 11.9 %collective-permute-start = (bf16[240,704]{0,1:T(8,128)(2,1)}, bf16[240,704]{0,1:T(8,128)(2,1)}, u32[]{:S(2)}, u32[]{:S(2)}) collective-permute-start(bf16[240,704]{0,1:T(8,128)(2,1)} %get-tuple-element.103), channel_id=1, source_target_pairs={{0,16},{8,24},{16,0},{24,8},{1,17},{9,25},{17,1},{25,9},{2,18},{10... | collective-permute-start | bytes 1013768 | tf_op jit(solution)/shard_map/ppermute | solution.py:48
  6.9 17.0 %collective-permute-start.21 = (bf16[256,960]{0,1:T(8,128)(2,1)}, bf16[256,960]{0,1:T(8,128)(2,1)S(1)}, u32[]{:S(2)}, u32[]{:S(2)}) collective-permute-start(bf16[256,960]{0,1:T(8,128)(2,1)} %bitcast.532), channel_id=1, source_target_pairs={{0,1},{1,0},{2,3},{3,2},{4,5},{5,4},{6,7},{7,6},{8,9},{9,8},{10,11... | collective-permute-start | bytes 1474568 | tf_op jit(solution)/shard_map/ppermute | solution.py:52
  16.3 21.6 %collective-permute-start.1 = (bf16[240,960]{1,0:T(8,128)(2,1)}, bf16[240,960]{1,0:T(8,128)(2,1)}, u32[]{:S(2)}, u32[]{:S(2)}) collective-permute-start(bf16[240,960]{1,0:T(8,128)(2,1)} %param.15), channel_id=1, source_target_pairs={{0,16},{8,24},{16,0},{24,8},{1,17},{9,25},{17,1},{25,9},{2,18},{10... | collective-permute-start | bytes 1382408 | tf_op jit(solution)/shard_map/ppermute | solution.py:48
  18.1 30.8 %collective-permute-start.6 = (bf16[240,960]{1,0:T(8,128)(2,1)}, bf16[240,960]{1,0:T(8,128)(2,1)}, u32[]{:S(2)}, u32[]{:S(2)}) collective-permute-start(bf16[240,960]{1,0:T(8,128)(2,1)} %param.15), channel_id=1, source_target_pairs={{0,8},{8,0},{16,24},{24,16},{1,9},{9,1},{17,25},{25,17},{2,10},{10... | collective-permute-start | bytes 1382408 | tf_op jit(solution)/shard_map/ppermute | solution.py:43
  19.2 5.8 %collective-permute-start.3 = (bf16[240,704]{0,1:T(8,128)(2,1)}, bf16[240,704]{0,1:T(8,128)(2,1)}, u32[]{:S(2)}, u32[]{:S(2)}) collective-permute-start(bf16[240,704]{0,1:T(8,128)(2,1)} %collective-permute-done), channel_id=1, source_target_pairs={{0,8},{8,0},{16,24},{24,16},{1,9},{9,1},{17,25},{25,17},{2,10},{10... | collective-permute-start | bytes 1013768 | tf_op jit(solution)/shard_map/ppermute | solution.py:43
  38.0 13.6 %collective-permute-start.5 = (bf16[256,640]{1,0:T(8,128)(2,1)S(1)}, bf16[256,640]{1,0:T(8,128)(2,1)S(1)}, u32[]{:S(2)}, u32[]{:S(2)}) collective-permute-start(bf16[256,640]{1,0:T(8,128)(2,1)S(1)} %pad_maximum_fusion.18), channel_id=1, source_target_pairs={{0,1},{1,0},{2,3},{3,2},{4,5},{5,4},{6,7},{7,6},{8,9},{9,8},{10,11... | collective-permute-start | bytes 983048 | tf_op jit(solution)/shard_map/ppermute | solution.py:52
  39.5 13.3 %collective-permute-start.8 = (bf16[256,640]{1,0:T(8,128)(2,1)S(1)}, bf16[256,640]{1,0:T(8,128)(2,1)}, u32[]{:S(2)}, u32[]{:S(2)}) collective-permute-start(bf16[256,640]{1,0:T(8,128)(2,1)S(1)} %pad_maximum_fusion.18), channel_id=1, source_target_pairs={{0,2},{2,4},{4,6},{1,3},{3,5},{5,7},{8,10},{10,12},{12,14},{9,11},... | collective-permute-start | bytes 983048 | tf_op jit(solution)/shard_map/ppermute | solution.py:58
  43.7 72.9 %collective-permute-start.4 = (bf16[240,3520]{1,0:T(8,128)(2,1)}, bf16[240,3520]{1,0:T(8,128)(2,1)}, u32[]{:S(2)}, u32[]{:S(2)}) collective-permute-start(bf16[240,3520]{1,0:T(8,128)(2,1)} %pad_maximum_fusion.2), channel_id=1, source_target_pairs={{0,16},{8,24},{16,0},{24,8},{1,17},{9,25},{17,1},{25,9},{2,18},{10... | collective-permute-start | bytes 5068808 | tf_op jit(solution)/shard_map/ppermute | solution.py:48
  44.2 74.2 %collective-permute-start.14 = (bf16[240,3520]{1,0:T(8,128)(2,1)}, bf16[240,3520]{1,0:T(8,128)(2,1)}, u32[]{:S(2)}, u32[]{:S(2)}) collective-permute-start(bf16[240,3520]{1,0:T(8,128)(2,1)} %pad_maximum_fusion.2), channel_id=1, source_target_pairs={{0,8},{8,0},{16,24},{24,16},{1,9},{9,1},{17,25},{25,17},{2,10},{10... | collective-permute-start | bytes 5068808 | tf_op jit(solution)/shard_map/ppermute | solution.py:43
  48.9 7.9 %collective-permute-start.7 = (bf16[240,960]{1,0:T(8,128)(2,1)}, bf16[240,960]{1,0:T(8,128)(2,1)}, u32[]{:S(2)}, u32[]{:S(2)}) collective-permute-start(bf16[240,960]{1,0:T(8,128)(2,1)} %collective-permute-done.1), channel_id=1, source_target_pairs={{0,8},{8,0},{16,24},{24,16},{1,9},{9,1},{17,25},{25,17},{2,10},{10... | collective-permute-start | bytes 1382408 | tf_op jit(solution)/shard_map/ppermute | solution.py:43
  52.7 15.5 %collective-permute-start.9 = (bf16[256,640]{1,0:T(8,128)(2,1)}, bf16[256,640]{1,0:T(8,128)(2,1)}, u32[]{:S(2)}, u32[]{:S(2)}) collective-permute-start(bf16[256,640]{1,0:T(8,128)(2,1)} %collective-permute-done.8), channel_id=1, source_target_pairs={{0,1},{1,0},{2,3},{3,2},{4,5},{5,4},{6,7},{7,6},{8,9},{9,8},{10,11... | collective-permute-start | bytes 983048 | tf_op jit(solution)/shard_map/ppermute | solution.py:52
  53.3 16.3 %collective-permute-start.10 = (bf16[256,640]{1,0:T(8,128)(2,1)}, bf16[256,640]{1,0:T(8,128)(2,1)}, u32[]{:S(2)}, u32[]{:S(2)}) collective-permute-start(bf16[256,640]{1,0:T(8,128)(2,1)} %collective-permute-done.8), channel_id=1, source_target_pairs={{0,2},{2,4},{4,6},{1,3},{3,5},{5,7},{8,10},{10,12},{12,14},{9,11},... | collective-permute-start | bytes 983048 | tf_op jit(solution)/shard_map/ppermute | solution.py:58
  69.6 9.6 %collective-permute-start.11 = (bf16[256,640]{1,0:T(8,128)(2,1)}, bf16[256,640]{1,0:T(8,128)(2,1)S(1)}, u32[]{:S(2)}, u32[]{:S(2)}) collective-permute-start(bf16[256,640]{1,0:T(8,128)(2,1)} %collective-permute-done.10), channel_id=1, source_target_pairs={{0,1},{1,0},{2,3},{3,2},{4,5},{5,4},{6,7},{7,6},{8,9},{9,8},{10,11... | collective-permute-start | bytes 983048 | tf_op jit(solution)/shard_map/ppermute | solution.py:52
  71.2 9.4 %collective-permute-start.12 = (bf16[256,640]{1,0:T(8,128)(2,1)}, bf16[256,640]{1,0:T(8,128)(2,1)S(1)}, u32[]{:S(2)}, u32[]{:S(2)}) collective-permute-start(bf16[256,640]{1,0:T(8,128)(2,1)} %collective-permute-done.10), channel_id=1, source_target_pairs={{0,2},{2,4},{4,6},{1,3},{3,5},{5,7},{8,10},{10,12},{12,14},{9,11},... | collective-permute-start | bytes 983048 | tf_op jit(solution)/shard_map/ppermute | solution.py:58
  80.5 8.6 %collective-permute-start.13 = (bf16[256,640]{1,0:T(8,128)(2,1)S(1)}, bf16[256,640]{1,0:T(8,128)(2,1)S(1)}, u32[]{:S(2)}, u32[]{:S(2)}) collective-permute-start(bf16[256,640]{1,0:T(8,128)(2,1)S(1)} %collective-permute-done.12), channel_id=1, source_target_pairs={{0,1},{1,0},{2,3},{3,2},{4,5},{5,4},{6,7},{7,6},{8,9},{9,8},{10,11... | collective-permute-start | bytes 983048 | tf_op jit(solution)/shard_map/ppermute | solution.py:52
  116.6 16.4 %collective-permute-start.17 = (bf16[240,1280]{1,0:T(8,128)(2,1)S(1)}, bf16[240,1280]{1,0:T(8,128)(2,1)S(1)}, u32[]{:S(2)}, u32[]{:S(2)}) collective-permute-start(bf16[240,1280]{1,0:T(8,128)(2,1)S(1)} %bitcast.540), channel_id=1, source_target_pairs={{0,8},{8,0},{16,24},{24,16},{1,9},{9,1},{17,25},{25,17},{2,10},{10... | collective-permute-start | bytes 1843208 | tf_op jit(solution)/shard_map/ppermute | solution.py:43
  116.7 16.3 %collective-permute-start.18 = (bf16[240,1280]{1,0:T(8,128)(2,1)S(1)}, bf16[240,1280]{1,0:T(8,128)(2,1)S(1)}, u32[]{:S(2)}, u32[]{:S(2)}) collective-permute-start(bf16[240,1280]{1,0:T(8,128)(2,1)S(1)} %bitcast.541), channel_id=1, source_target_pairs={{0,16},{8,24},{16,0},{24,8},{1,17},{9,25},{17,1},{25,9},{2,18},{10... | collective-permute-start | bytes 1843208 | tf_op jit(solution)/shard_map/ppermute | solution.py:48
  118.3 14.8 %collective-permute-start.15 = (bf16[240,3520]{1,0:T(8,128)(2,1)}, bf16[240,3520]{1,0:T(8,128)(2,1)S(1)}, u32[]{:S(2)}, u32[]{:S(2)}) collective-permute-start(bf16[240,3520]{1,0:T(8,128)(2,1)} %collective-permute-done.4), channel_id=1, source_target_pairs={{0,8},{8,0},{16,24},{24,16},{1,9},{9,1},{17,25},{25,17},{2,10},{10... | collective-permute-start | bytes 5068808 | tf_op jit(solution)/shard_map/ppermute | solution.py:43
  133.0 5.2 %collective-permute-start.19 = (bf16[240,1280]{1,0:T(8,128)(2,1)S(1)}, bf16[240,1280]{1,0:T(8,128)(2,1)S(1)}, u32[]{:S(2)}, u32[]{:S(2)}) collective-permute-start(bf16[240,1280]{1,0:T(8,128)(2,1)S(1)} %collective-permute-done.18), channel_id=1, source_target_pairs={{0,8},{8,0},{16,24},{24,16},{1,9},{9,1},{17,25},{25,17},{2,10},{10... | collective-permute-start | bytes 1843208 | tf_op jit(solution)/shard_map/ppermute | solution.py:43
  137.1 13.7 %collective-permute-start.16 = (bf16[256,960]{0,1:T(8,128)(2,1)S(1)}, bf16[256,960]{0,1:T(8,128)(2,1)S(1)}, u32[]{:S(2)}, u32[]{:S(2)}) collective-permute-start(bf16[256,960]{0,1:T(8,128)(2,1)S(1)} %multiply_convert_fusion.3), channel_id=1, source_target_pairs={{0,1},{1,0},{2,3},{3,2},{4,5},{5,4},{6,7},{7,6},{8,9},{9,8},{10,11... | collective-permute-start | bytes 1474568 | tf_op jit(solution)/shard_map/ppermute | solution.py:52
  170.7 24.5 %collective-permute-start.20 = (bf16[256,960]{0,1:T(8,128)(2,1)S(1)}, bf16[256,960]{0,1:T(8,128)(2,1)S(1)}, u32[]{:S(2)}, u32[]{:S(2)}) collective-permute-start(bf16[256,960]{0,1:T(8,128)(2,1)S(1)} %slice.551), channel_id=1, source_target_pairs={{0,1},{1,0},{2,3},{3,2},{4,5},{5,4},{6,7},{7,6},{8,9},{9,8},{10,11... | collective-permute-start | bytes 1474568 | tf_op jit(solution)/shard_map/ppermute | solution.py:52
  171.8 22.4 %collective-permute-start.22 = (bf16[256,960]{0,1:T(8,128)(2,1)}, bf16[256,960]{0,1:T(8,128)(2,1)S(1)}, u32[]{:S(2)}, u32[]{:S(2)}) collective-permute-start(bf16[256,960]{0,1:T(8,128)(2,1)} %fusion.100), channel_id=1, source_target_pairs={{0,1},{1,0},{2,3},{3,2},{4,5},{5,4},{6,7},{7,6},{8,9},{9,8},{10,11... | collective-permute-start | bytes 1474568 | tf_op jit(solution)/shard_map/ppermute | solution.py:52
  229.7 49.1 %collective-permute-start.59 = (bf16[2,240,1280]{2,1,0:T(8,128)(2,1)S(1)}, bf16[2,240,1280]{2,1,0:T(8,128)(2,1)S(1)}, u32[]{:S(2)}, u32[]{:S(2)}) collective-permute-start(bf16[2,240,1280]{2,1,0:T(8,128)(2,1)S(1)} %slice_bitcast_fusion.4), channel_id=1, source_target_pairs={{0,8},{8,0},{16,24},{24,16},{1,9},{9,1},{17,25},{25,17},{2,10},{10... | collective-permute-start | bytes 3686408 | tf_op jit(solution)/shard_map/ppermute | solution.py:43
  231.7 30.9 %collective-permute-start.44 = (bf16[2,240,960]{2,1,0:T(8,128)(2,1)S(1)}, bf16[2,240,960]{2,1,0:T(8,128)(2,1)S(1)}, u32[]{:S(2)}, u32[]{:S(2)}) collective-permute-start(bf16[2,240,960]{2,1,0:T(8,128)(2,1)S(1)} %slice_bitcast_fusion.7), channel_id=1, source_target_pairs={{0,8},{8,0},{16,24},{24,16},{1,9},{9,1},{17,25},{25,17},{2,10},{10... | collective-permute-start | bytes 2764808 | tf_op jit(solution)/shard_map/ppermute | solution.py:43
  233.4 19.9 %collective-permute-start.25 = (bf16[256,640]{0,1:T(8,128)(2,1)S(1)}, bf16[256,640]{0,1:T(8,128)(2,1)S(1)}, u32[]{:S(2)}, u32[]{:S(2)}) collective-permute-start(bf16[256,640]{0,1:T(8,128)(2,1)S(1)} %fusion.167), channel_id=1, source_target_pairs={{0,1},{1,0},{2,3},{3,2},{4,5},{5,4},{6,7},{7,6},{8,9},{9,8},{10,11... | collective-permute-start | bytes 983048 | tf_op jit(solution)/shard_map/ppermute | solution.py:52
  234.5 15.8 %collective-permute-start.26 = (bf16[256,640]{0,1:T(8,128)(2,1)S(1)}, bf16[256,640]{0,1:T(8,128)(2,1)S(1)}, u32[]{:S(2)}, u32[]{:S(2)}) collective-permute-start(bf16[256,640]{0,1:T(8,128)(2,1)S(1)} %fusion.166), channel_id=1, source_target_pairs={{0,1},{1,0},{2,3},{3,2},{4,5},{5,4},{6,7},{7,6},{8,9},{9,8},{10,11... | collective-permute-start | bytes 983048 | tf_op jit(solution)/shard_map/ppermute | solution.py:52
  240.6 23.5 %collective-permute-start.37 = (bf16[2,240,960]{2,1,0:T(8,128)(2,1)S(1)}, bf16[2,240,960]{2,1,0:T(8,128)(2,1)S(1)}, u32[]{:S(2)}, u32[]{:S(2)}) collective-permute-start(bf16[2,240,960]{2,1,0:T(8,128)(2,1)S(1)} %slice_bitcast_fusion.10), channel_id=1, source_target_pairs={{0,8},{8,0},{16,24},{24,16},{1,9},{9,1},{17,25},{25,17},{2,10},{10... | collective-permute-start | bytes 2764808 | tf_op jit(solution)/shard_map/ppermute | solution.py:43
  250.5 11.0 %collective-permute-start.27 = (bf16[256,640]{0,1:T(8,128)(2,1)S(1)}, bf16[256,640]{0,1:T(8,128)(2,1)S(1)}, u32[]{:S(2)}, u32[]{:S(2)}) collective-permute-start(bf16[256,640]{0,1:T(8,128)(2,1)S(1)} %fusion.154), channel_id=1, source_target_pairs={{2,0},{4,2},{6,4},{3,1},{5,3},{7,5},{10,8},{12,10},{14,12},{11,9},... | collective-permute-start | bytes 983048 | tf_op jit(solution)/shard_map/ppermute | solution.py:58
  253.3 96.1 %collective-permute-start.51 = (bf16[2,240,2560]{2,1,0:T(8,128)(2,1)}, bf16[2,240,2560]{2,1,0:T(8,128)(2,1)}, u32[]{:S(2)}, u32[]{:S(2)}) collective-permute-start(bf16[2,240,2560]{2,1,0:T(8,128)(2,1)} %slice_bitcast_fusion.1), channel_id=1, source_target_pairs={{0,8},{8,0},{16,24},{24,16},{1,9},{9,1},{17,25},{25,17},{2,10},{10... | collective-permute-start | bytes 7372808 | tf_op jit(solution)/shard_map/ppermute | solution.py:43
  261.5 19.9 %collective-permute-start.23 = (bf16[256,640]{0,1:T(8,128)(2,1)S(1)}, bf16[256,640]{0,1:T(8,128)(2,1)S(1)}, u32[]{:S(2)}, u32[]{:S(2)}) collective-permute-start(bf16[256,640]{0,1:T(8,128)(2,1)S(1)} %fusion.169), channel_id=1, source_target_pairs={{0,1},{1,0},{2,3},{3,2},{4,5},{5,4},{6,7},{7,6},{8,9},{9,8},{10,11... | collective-permute-start | bytes 983048 | tf_op jit(solution)/shard_map/ppermute | solution.py:52
  262.6 14.0 %collective-permute-start.24 = (bf16[256,640]{0,1:T(8,128)(2,1)S(1)}, bf16[256,640]{0,1:T(8,128)(2,1)S(1)}, u32[]{:S(2)}, u32[]{:S(2)}) collective-permute-start(bf16[256,640]{0,1:T(8,128)(2,1)S(1)} %fusion.168), channel_id=1, source_target_pairs={{0,1},{1,0},{2,3},{3,2},{4,5},{5,4},{6,7},{7,6},{8,9},{9,8},{10,11... | collective-permute-start | bytes 983048 | tf_op jit(solution)/shard_map/ppermute | solution.py:52
  264.1 14.0 %collective-permute-start.28 = (bf16[256,640]{0,1:T(8,128)(2,1)S(1)}, bf16[256,640]{0,1:T(8,128)(2,1)S(1)}, u32[]{:S(2)}, u32[]{:S(2)}) collective-permute-start(bf16[256,640]{0,1:T(8,128)(2,1)S(1)} %fusion.158), channel_id=1, source_target_pairs={{2,0},{4,2},{6,4},{3,1},{5,3},{7,5},{10,8},{12,10},{14,12},{11,9},... | collective-permute-start | bytes 983048 | tf_op jit(solution)/shard_map/ppermute | solution.py:58
  276.6 26.8 %collective-permute-start.45 = (bf16[240,960]{1,0:T(8,128)(2,1)}, bf16[240,960]{1,0:T(8,128)(2,1)}, u32[]{:S(2)}, u32[]{:S(2)}) collective-permute-start(bf16[240,960]{1,0:T(8,128)(2,1)} %fusion.173), channel_id=1, source_target_pairs={{0,16},{8,24},{16,0},{24,8},{1,17},{9,25},{17,1},{25,9},{2,18},{10... | collective-permute-start | bytes 1382408 | tf_op jit(solution)/shard_map/ppermute | solution.py:48
  278.1 28.0 %collective-permute-start.38 = (bf16[240,960]{1,0:T(8,128)(2,1)}, bf16[240,960]{1,0:T(8,128)(2,1)}, u32[]{:S(2)}, u32[]{:S(2)}) collective-permute-start(bf16[240,960]{1,0:T(8,128)(2,1)} %fusion.172), channel_id=1, source_target_pairs={{0,16},{8,24},{16,0},{24,8},{1,17},{9,25},{17,1},{25,9},{2,18},{10... | collective-permute-start | bytes 1382408 | tf_op jit(solution)/shard_map/ppermute | solution.py:48
  278.8 9.0 %collective-permute-start.29 = (bf16[256,640]{0,1:T(8,128)(2,1)S(1)}, bf16[256,640]{0,1:T(8,128)(2,1)S(1)}, u32[]{:S(2)}, u32[]{:S(2)}) collective-permute-start(bf16[256,640]{0,1:T(8,128)(2,1)S(1)} %fusion.162), channel_id=1, source_target_pairs={{2,0},{4,2},{6,4},{3,1},{5,3},{7,5},{10,8},{12,10},{14,12},{11,9},... | collective-permute-start | bytes 983048 | tf_op jit(solution)/shard_map/ppermute | solution.py:58
  281.4 41.1 %collective-permute-start.60 = (bf16[240,1280]{1,0:T(8,128)(2,1)}, bf16[240,1280]{1,0:T(8,128)(2,1)}, u32[]{:S(2)}, u32[]{:S(2)}) collective-permute-start(bf16[240,1280]{1,0:T(8,128)(2,1)} %fusion.170), channel_id=1, source_target_pairs={{0,16},{8,24},{16,0},{24,8},{1,17},{9,25},{17,1},{25,9},{2,18},{10... | collective-permute-start | bytes 1843208 | tf_op jit(solution)/shard_map/ppermute | solution.py:48
  299.5 30.3 %collective-permute-start.30 = (bf16[2,240,704]{1,2,0:T(8,128)(2,1)}, bf16[2,240,704]{1,2,0:T(8,128)(2,1)}, u32[]{:S(2)}, u32[]{:S(2)}) collective-permute-start(bf16[2,240,704]{1,2,0:T(8,128)(2,1)} %bitcast.538), channel_id=1, source_target_pairs={{0,8},{8,0},{16,24},{24,16},{1,9},{9,1},{17,25},{25,17},{2,10},{10... | collective-permute-start | bytes 2027528 | tf_op jit(solution)/shard_map/ppermute | solution.py:43
  305.1 8.8 %collective-permute-start.46 = (bf16[120,960]{1,0:T(8,128)(2,1)S(1)}, bf16[120,960]{1,0:T(8,128)(2,1)S(1)}, u32[]{:S(2)}, u32[]{:S(2)}) collective-permute-start(bf16[120,960]{1,0:T(8,128)(2,1)S(1)} %dynamic-slice_convert_fusion), channel_id=1, source_target_pairs={{0,1},{1,0},{2,3},{3,2},{4,5},{5,4},{6,7},{7,6},{8,9},{9,8},{10,11... | collective-permute-start | bytes 691208 | tf_op jit(solution)/shard_map/ppermute | solution.py:52
  307.3 11.4 %collective-permute-start.39 = (bf16[120,960]{1,0:T(8,128)(2,1)S(1)}, bf16[120,960]{1,0:T(8,128)(2,1)S(1)}, u32[]{:S(2)}, u32[]{:S(2)}) collective-permute-start(bf16[120,960]{1,0:T(8,128)(2,1)S(1)} %dynamic-slice_convert_fusion.1), channel_id=1, source_target_pairs={{0,1},{1,0},{2,3},{3,2},{4,5},{5,4},{6,7},{7,6},{8,9},{9,8},{10,11... | collective-permute-start | bytes 691208 | tf_op jit(solution)/shard_map/ppermute | solution.py:52
  314.0 11.3 %collective-permute-start.47 = (bf16[120,960]{1,0:T(8,128)(2,1)S(1)}, bf16[120,960]{1,0:T(8,128)(2,1)S(1)}, u32[]{:S(2)}, u32[]{:S(2)}) collective-permute-start(bf16[120,960]{1,0:T(8,128)(2,1)S(1)} %fusion.188), channel_id=1, source_target_pairs={{0,2},{6,4},{1,3},{7,5},{8,10},{14,12},{9,11},{15,13},{16,18},{22,... | collective-permute-start | bytes 691208 | tf_op jit(solution)/shard_map/ppermute | solution.py:108
  318.8 10.0 %collective-permute-start.40 = (bf16[120,960]{1,0:T(8,128)(2,1)S(1)}, bf16[120,960]{1,0:T(8,128)(2,1)S(1)}, u32[]{:S(2)}, u32[]{:S(2)}) collective-permute-start(bf16[120,960]{1,0:T(8,128)(2,1)S(1)} %fusion.187), channel_id=1, source_target_pairs={{0,2},{6,4},{1,3},{7,5},{8,10},{14,12},{9,11},{15,13},{16,18},{22,... | collective-permute-start | bytes 691208 | tf_op jit(solution)/shard_map/ppermute | solution.py:108
  323.8 29.1 %collective-permute-start.61 = (bf16[240,1280]{1,0:T(8,128)(2,1)S(1)}, bf16[240,1280]{1,0:T(8,128)(2,1)S(1)}, u32[]{:S(2)}, u32[]{:S(2)}) collective-permute-start(bf16[240,1280]{1,0:T(8,128)(2,1)S(1)} %fusion.150), channel_id=1, source_target_pairs={{0,2},{6,4},{1,3},{7,5},{8,10},{14,12},{9,11},{15,13},{16,18},{22,... | collective-permute-start | bytes 1843208 | tf_op jit(solution)/shard_map/ppermute | solution.py:108
  325.4 7.2 %collective-permute-start.48 = (bf16[120,960]{1,0:T(8,128)(2,1)S(1)}, bf16[120,960]{1,0:T(8,128)(2,1)S(1)}, u32[]{:S(2)}, u32[]{:S(2)}) collective-permute-start(bf16[120,960]{1,0:T(8,128)(2,1)S(1)} %add_convert_fusion.7), channel_id=1, source_target_pairs={{2,4},{4,2},{3,5},{5,3},{10,12},{12,10},{11,13},{13,11},{18,20},{2... | collective-permute-start | bytes 691208 | tf_op jit(solution)/shard_map/ppermute | solution.py:110
  328.9 5.1 %collective-permute-start.41 = (bf16[120,960]{1,0:T(8,128)(2,1)S(1)}, bf16[120,960]{1,0:T(8,128)(2,1)S(1)}, u32[]{:S(2)}, u32[]{:S(2)}) collective-permute-start(bf16[120,960]{1,0:T(8,128)(2,1)S(1)} %add_convert_fusion.9), channel_id=1, source_target_pairs={{2,4},{4,2},{3,5},{5,3},{10,12},{12,10},{11,13},{13,11},{18,20},{2... | collective-permute-start | bytes 691208 | tf_op jit(solution)/shard_map/ppermute | solution.py:110
  331.1 16.6 %collective-permute-start.31 = (bf16[240,704]{0,1:T(8,128)(2,1)S(1)}, bf16[240,704]{0,1:T(8,128)(2,1)S(1)}, u32[]{:S(2)}, u32[]{:S(2)}) collective-permute-start(bf16[240,704]{0,1:T(8,128)(2,1)S(1)} %fusion.186), channel_id=1, source_target_pairs={{0,16},{8,24},{16,0},{24,8},{1,17},{9,25},{17,1},{25,9},{2,18},{10... | collective-permute-start | bytes 1013768 | tf_op jit(solution)/shard_map/ppermute | solution.py:48
  332.7 11.7 %collective-permute-start.49 = (bf16[120,960]{1,0:T(8,128)(2,1)S(1)}, bf16[120,960]{1,0:T(8,128)(2,1)S(1)}, u32[]{:S(2)}, u32[]{:S(2)}) collective-permute-start(bf16[120,960]{1,0:T(8,128)(2,1)S(1)} %add_convert_fusion.6), channel_id=1, source_target_pairs={{2,0},{4,6},{3,1},{5,7},{10,8},{12,14},{11,9},{13,15},{18,16},{20,... | collective-permute-start | bytes 691208 | tf_op jit(solution)/shard_map/ppermute | solution.py:112
  334.1 13.0 %collective-permute-start.42 = (bf16[120,960]{1,0:T(8,128)(2,1)S(1)}, bf16[120,960]{1,0:T(8,128)(2,1)S(1)}, u32[]{:S(2)}, u32[]{:S(2)}) collective-permute-start(bf16[120,960]{1,0:T(8,128)(2,1)S(1)} %add_convert_fusion.8), channel_id=1, source_target_pairs={{2,0},{4,6},{3,1},{5,7},{10,8},{12,14},{11,9},{13,15},{18,16},{20,... | collective-permute-start | bytes 691208 | tf_op jit(solution)/shard_map/ppermute | solution.py:112
  344.5 15.6 %collective-permute-start.50 = (bf16[120,960]{1,0:T(8,128)(2,1)S(1)}, bf16[120,960]{1,0:T(8,128)(2,1)S(1)}, u32[]{:S(2)}, u32[]{:S(2)}) collective-permute-start(bf16[120,960]{1,0:T(8,128)(2,1)S(1)} %broadcast_select_fusion), channel_id=1, source_target_pairs={{0,1},{1,0},{2,3},{3,2},{4,5},{5,4},{6,7},{7,6},{8,9},{9,8},{10,11... | collective-permute-start | bytes 691208 | tf_op jit(solution)/shard_map/ppermute | solution.py:52
  347.1 13.0 %collective-permute-start.43 = (bf16[120,960]{1,0:T(8,128)(2,1)S(1)}, bf16[120,960]{1,0:T(8,128)(2,1)S(1)}, u32[]{:S(2)}, u32[]{:S(2)}) collective-permute-start(bf16[120,960]{1,0:T(8,128)(2,1)S(1)} %broadcast_select_fusion.1), channel_id=1, source_target_pairs={{0,1},{1,0},{2,3},{3,2},{4,5},{5,4},{6,7},{7,6},{8,9},{9,8},{10,11... | collective-permute-start | bytes 691208 | tf_op jit(solution)/shard_map/ppermute | solution.py:52
  347.9 10.5 %collective-permute-start.32 = (bf16[120,704]{0,1:T(8,128)(2,1)S(1)}, bf16[120,704]{0,1:T(8,128)(2,1)S(1)}, u32[]{:S(2)}, u32[]{:S(2)}) collective-permute-start(bf16[120,704]{0,1:T(8,128)(2,1)S(1)} %dynamic-slice_convert_fusion.2), channel_id=1, source_target_pairs={{0,1},{1,0},{2,3},{3,2},{4,5},{5,4},{6,7},{7,6},{8,9},{9,8},{10,11... | collective-permute-start | bytes 506888 | tf_op jit(solution)/shard_map/ppermute | solution.py:52
  352.0 25.6 %collective-permute-start.52 = (bf16[240,2560]{1,0:T(8,128)(2,1)S(1)}, bf16[240,2560]{1,0:T(8,128)(2,1)S(1)}, u32[]{:S(2)}, u32[]{:S(2)}) collective-permute-start(bf16[240,2560]{1,0:T(8,128)(2,1)S(1)} %fusion.105), channel_id=1, source_target_pairs={{0,16},{8,24},{16,0},{24,8},{1,17},{9,25},{17,1},{25,9},{2,18},{10... | collective-permute-start | bytes 3686408 | tf_op jit(solution)/shard_map/ppermute | solution.py:48
  354.3 48.6 %collective-permute-start.62 = (bf16[240,1280]{1,0:T(8,128)(2,1)S(1)}, bf16[240,1280]{1,0:T(8,128)(2,1)S(1)}, u32[]{:S(2)}, u32[]{:S(2)}) collective-permute-start(bf16[240,1280]{1,0:T(8,128)(2,1)S(1)} %add_convert_fusion.1), channel_id=1, source_target_pairs={{2,4},{4,2},{3,5},{5,3},{10,12},{12,10},{11,13},{13,11},{18,20},{2... | collective-permute-start | bytes 1843208 | tf_op jit(solution)/shard_map/ppermute | solution.py:110
  358.6 4.5 collective-permute-start.33
  363.2 17.7 %collective-permute-start.34 = (bf16[120,704]{0,1:T(8,128)(2,1)S(1)}, bf16[120,704]{0,1:T(8,128)(2,1)S(1)}, u32[]{:S(2)}, u32[]{:S(2)}) collective-permute-start(bf16[120,704]{0,1:T(8,128)(2,1)S(1)} %add_convert_fusion.12), channel_id=1, source_target_pairs={{2,4},{4,2},{3,5},{5,3},{10,12},{12,10},{11,13},{13,11},{18,20},{2... | collective-permute-start | bytes 506888 | tf_op jit(solution)/shard_map/ppermute | solution.py:110
  378.1 15.7 %collective-permute-start.53 = (bf16[240,1280]{1,0:T(8,128)(2,1)S(1)}, bf16[240,1280]{1,0:T(8,128)(2,1)S(1)}, u32[]{:S(2)}, u32[]{:S(2)}) collective-permute-start(bf16[240,1280]{1,0:T(8,128)(2,1)S(1)} %get-tuple-element.63), channel_id=1, source_target_pairs={{0,2},{6,4},{1,3},{7,5},{8,10},{14,12},{9,11},{15,13},{16,18},{22,... | collective-permute-start | bytes 1843208 | tf_op jit(solution)/shard_map/ppermute | solution.py:108
  379.6 22.3 %collective-permute-start.56 = (bf16[240,1280]{1,0:T(8,128)(2,1)S(1)}, bf16[240,1280]{1,0:T(8,128)(2,1)S(1)}, u32[]{:S(2)}, u32[]{:S(2)}) collective-permute-start(bf16[240,1280]{1,0:T(8,128)(2,1)S(1)} %get-tuple-element.62), channel_id=1, source_target_pairs={{0,2},{6,4},{1,3},{7,5},{8,10},{14,12},{9,11},{15,13},{16,18},{22,... | collective-permute-start | bytes 1843208 | tf_op jit(solution)/shard_map/ppermute | solution.py:108
  381.0 7.4 %collective-permute-start.35 = (bf16[120,704]{0,1:T(8,128)(2,1)S(1)}, bf16[120,704]{0,1:T(8,128)(2,1)S(1)}, u32[]{:S(2)}, u32[]{:S(2)}) collective-permute-start(bf16[120,704]{0,1:T(8,128)(2,1)S(1)} %add_convert_fusion.11), channel_id=1, source_target_pairs={{2,0},{4,6},{3,1},{5,7},{10,8},{12,14},{11,9},{13,15},{18,16},{20,... | collective-permute-start | bytes 506888 | tf_op jit(solution)/shard_map/ppermute | solution.py:112
  388.4 16.0 %collective-permute-start.36 = (bf16[120,704]{0,1:T(8,128)(2,1)S(1)}, bf16[120,704]{0,1:T(8,128)(2,1)S(1)}, u32[]{:S(2)}, u32[]{:S(2)}) collective-permute-start(bf16[120,704]{0,1:T(8,128)(2,1)S(1)} %broadcast_select_fusion.6), channel_id=1, source_target_pairs={{0,1},{1,0},{2,3},{3,2},{4,5},{5,4},{6,7},{7,6},{8,9},{9,8},{10,11... | collective-permute-start | bytes 506888 | tf_op jit(solution)/shard_map/ppermute | solution.py:52
  402.2 4.6 %collective-permute-start.57 = (bf16[240,1280]{1,0:T(8,128)(2,1)S(1)}, bf16[240,1280]{1,0:T(8,128)(2,1)S(1)}, u32[]{:S(2)}, u32[]{:S(2)}) collective-permute-start(bf16[240,1280]{1,0:T(8,128)(2,1)S(1)} %get-tuple-element.60), channel_id=1, source_target_pairs={{2,4},{4,2},{3,5},{5,3},{10,12},{12,10},{11,13},{13,11},{18,20},{2... | collective-permute-start | bytes 1843208 | tf_op jit(solution)/shard_map/ppermute | solution.py:110
  403.0 17.3 %collective-permute-start.63 = (bf16[240,1280]{1,0:T(8,128)(2,1)S(1)}, bf16[240,1280]{1,0:T(8,128)(2,1)S(1)}, u32[]{:S(2)}, u32[]{:S(2)}) collective-permute-start(bf16[240,1280]{1,0:T(8,128)(2,1)S(1)} %add_convert_fusion), channel_id=1, source_target_pairs={{2,0},{4,6},{3,1},{5,7},{10,8},{12,14},{11,9},{13,15},{18,16},{20,... | collective-permute-start | bytes 1843208 | tf_op jit(solution)/shard_map/ppermute | solution.py:112
  405.4 2.8 collective-permute-start.54
  406.9 32.2 %collective-permute-start.58 = (bf16[240,1280]{1,0:T(8,128)(2,1)S(1)}, bf16[240,1280]{1,0:T(8,128)(2,1)S(1)}, u32[]{:S(2)}, u32[]{:S(2)}) collective-permute-start(bf16[240,1280]{1,0:T(8,128)(2,1)S(1)} %add_convert_fusion.2), channel_id=1, source_target_pairs={{2,0},{4,6},{3,1},{5,7},{10,8},{12,14},{11,9},{13,15},{18,16},{20,... | collective-permute-start | bytes 1843208 | tf_op jit(solution)/shard_map/ppermute | solution.py:112
  408.3 37.7 %collective-permute-start.55 = (bf16[240,1280]{1,0:T(8,128)(2,1)S(1)}, bf16[240,1280]{1,0:T(8,128)(2,1)S(1)}, u32[]{:S(2)}, u32[]{:S(2)}) collective-permute-start(bf16[240,1280]{1,0:T(8,128)(2,1)S(1)} %add_convert_fusion.4), channel_id=1, source_target_pairs={{2,0},{4,6},{3,1},{5,7},{10,8},{12,14},{11,9},{13,15},{18,16},{20,... | collective-permute-start | bytes 1843208 | tf_op jit(solution)/shard_map/ppermute | solution.py:112
  (93 other events, 534.7 us)
